TPU v7x, 32 devices: a whole 2x2x4 slice. The times are simulated.
32 devices in a mesh: seq: 8 (over z, y), head: 4 (over x, core).
Axes of the slice: x: 2, y: 2, z: 4, core: 2. Of those that a mesh axis runs over, the one named last changes fastest.
Arguments:
- inner_input: bfloat16 [2048, 8192], P('seq', 'head'), may hold values from -6 to 6
- state_input: bfloat16 [2048, 2, 1024], P('seq', None, 'head'), may hold values from -3 to 3
- gate_input: bfloat16 [2048, 8192], P('seq', 'head'), may hold values from -6 to 6
- step_input: float32 [128, 2048], P('head', 'seq'), may hold values from -4.7 to 0.6
- decay_exponent: float32 [128], P('head')
- skip_gain: float32 [128], P('head'), may hold values from 0.5 to 1.5
- documents: int32 [2048], P('seq'), may hold values from 0 to 1, never falling along the last dimension, each value on 1 to 1536 neighbouring positions
- filter_inner: float32 [4, 8192], P(None, 'head'), may hold values from -3 to 3
- filter_state: float32 [4, 2, 1024], P(None, None, 'head'), may hold values from -3 to 3
- norm_gain: float32 [8192], P('head'), may hold values from 0.1 to 1.9
- output_weight: bfloat16 [8192, 4096], P('head', 'seq'), may hold values from -0.0625 to 0.0625
Outputs:
- mixed: bfloat16 [2048, 4096], P('seq', 'head')
Inputs may be any that keep to these rules, and one draw needn't show every extreme that they name: `documents`: document numbers never fall along the sequence.
All inputs are finite; a program needn't handle non-finite values.
Results may differ from a plain program's by a relative error of at most 0.0058.
Values may be sent and summed in bfloat16 or wider, within the bound.
A program may use at most 192 MiB of HBM per device.

v0:
```python
import jax
import jax.numpy as jnp
from jax import lax
from jax.sharding import PartitionSpec as P

HEAD_DIM = 64
STATE = 128
GROUPS = 8
INNER = 8192
KERNEL = 4


highest = lax.Precision.HIGHEST


def entering(part, axis, combine, identity):
    place = lax.axis_index(axis)
    gathered = jax.tree.map(lambda a: lax.all_gather(a, axis), part)
    state = jax.tree.map(lambda a, e: jnp.zeros_like(a) + jnp.asarray(e, a.dtype), part, identity)

    def one(step, state):
        return combine(
            state, jax.tree.map(lambda a: lax.dynamic_index_in_dim(a, step, 0, False), gathered)
        )

    return lax.fori_loop(0, place, one, state)


def passed_along(value, axis, steps):
    count = lax.axis_size(axis)
    initial, last = (max(0, -steps), min(count, count - steps))
    return lax.ppermute(value, axis, [(source, source + steps) for source in range(initial, last)])


def causal_conv(extended, weights, segments_wide, segment_block):
    length = segment_block.shape[0]
    running = jnp.zeros(extended[:length].shape, jnp.float32)
    for offset in range(KERNEL):
        window = extended[offset : offset + length].astype(jnp.float32)
        matches = segments_wide[offset : offset + length] == segment_block
        matches = matches.reshape((length,) + (1,) * (extended.ndim - 1))
        running = running + jnp.where(matches, window * weights[offset], jnp.float32(0.0))
    return jax.nn.silu(running).astype(jnp.bfloat16)


def span_parts(values, write_rows, read_rows, step_size, decay_rate, segment_block, prior_segment):
    length = segment_block.shape[0]
    repeat = decay_rate.shape[0] // write_rows.shape[1]
    cumulative = jnp.cumsum(decay_rate, axis=1)
    places = jnp.arange(length)
    linked = (segment_block[:, None] == segment_block[None, :]) & (
        places[:, None] >= places[None, :]
    )
    spread = cumulative[:, :, None] - cumulative[:, None, :]
    decays = jnp.exp(jnp.where(linked[None], spread, -jnp.inf))
    scores = jnp.einsum("ign,jgn->gij", read_rows, write_rows, preferred_element_type=jnp.float32)
    scores = jnp.repeat(scores, repeat, axis=0)
    mixing = (decays * scores * step_size[:, None, :]).astype(jnp.bfloat16)
    within = jnp.einsum("hij,jhp->ihp", mixing, values, preferred_element_type=jnp.float32)
    inflow = jnp.exp(cumulative) * (segment_block == prior_segment)[None, :].astype(jnp.float32)
    final_segment = segment_block[-1]
    closing = (
        jnp.exp(cumulative[:, -1:] - cumulative)
        * (segment_block == final_segment)[None, :].astype(jnp.float32)
        * step_size
    )
    weighted = (values.astype(jnp.float32) * closing.T[:, :, None]).astype(jnp.bfloat16)
    writes = jnp.repeat(write_rows, repeat, axis=1)
    deposit = jnp.einsum("jhp,jhn->hpn", weighted, writes, preferred_element_type=jnp.float32)
    fading = jnp.exp(cumulative[:, -1]) * (final_segment == prior_segment).astype(jnp.float32)
    return (within, inflow, fading, deposit)


def reading(read_rows, held_state, repeat):
    readers = jnp.repeat(read_rows, repeat, axis=1).astype(jnp.float32)
    return jnp.einsum("ihn,hpn->ihp", readers, held_state, precision=highest)


def gated_norm(outputs, gates, norm_scale):
    height = outputs.shape[0]
    gated = outputs * jax.nn.silu(gates.astype(jnp.float32))
    grouped = gated.reshape(height, -1, INNER // GROUPS)
    mean_square = jnp.mean(grouped * grouped, axis=-1, keepdims=True)
    normed = (grouped * lax.rsqrt(mean_square + 1e-05)).reshape(height, -1) * norm_scale
    return normed.astype(jnp.bfloat16)


def chain_states(through, local_state):

    def combine_pair(earlier, later):
        return (earlier[0] * later[0], later[0][:, None, None] * earlier[1] + later[1])

    neutral = (jnp.ones_like(through), jnp.zeros_like(local_state))
    return entering((through, local_state), "seq", combine_pair, neutral)[1]


def on_device(
    inner_input,
    state_input,
    gate_input,
    step_input,
    decay_exponent,
    skip_gain,
    documents,
    filter_inner,
    filter_state,
    norm_gain,
    output_weight,
):
    margin = KERNEL - 1
    length = documents.shape[0]
    head_count = decay_exponent.shape[0]
    groups = state_input.shape[2] // STATE
    repeat = head_count // groups
    before_inner, before_state, before_segments = passed_along(
        (inner_input[-margin:], state_input[-margin:], documents[-margin:].astype(jnp.bfloat16)),
        "seq",
        1,
    )
    segments_wide = jnp.concatenate([before_segments.astype(jnp.int32), documents])
    inner_conv = causal_conv(
        jnp.concatenate([before_inner, inner_input]), filter_inner, segments_wide, documents
    )
    state_conv = causal_conv(
        jnp.concatenate([before_state, state_input]), filter_state, segments_wide, documents
    )
    values = inner_conv.reshape(length, head_count, HEAD_DIM)
    write_rows = state_conv[:, 0].reshape(length, groups, STATE)
    read_rows = state_conv[:, 1].reshape(length, groups, STATE)
    step_size = jax.nn.softplus(step_input)
    decay_rate = -step_size * jnp.exp(decay_exponent)[:, None]
    skipped = skip_gain[None, :, None] * values.astype(jnp.float32)
    prior_segment = segments_wide[margin - 1]
    pieces = [
        span_parts(values, write_rows, read_rows, step_size, decay_rate, documents, prior_segment)
    ]
    local_state = jnp.zeros((head_count, HEAD_DIM, STATE), jnp.float32)
    through = jnp.ones((head_count,), jnp.float32)
    block_index = 0
    within, inflow, fading, deposit = pieces[block_index]
    local_state = fading[:, None, None] * local_state + deposit
    through = through * fading
    carried = chain_states(through, local_state)
    block_index = 0
    within, inflow, fading, deposit = pieces[block_index]
    outputs = within + inflow.T[:, :, None] * reading(read_rows, carried, repeat) + skipped
    scan_out = outputs.reshape(length, head_count * HEAD_DIM)
    normed = gated_norm(scan_out, gate_input, norm_gain)
    partial_value = jnp.dot(
        normed,
        lax.all_gather(output_weight, "seq", axis=1, tiled=True),
        preferred_element_type=jnp.float32,
    )
    return lax.psum_scatter(partial_value, "head", scatter_dimension=1, tiled=True).astype(
        jnp.bfloat16
    )


def solution(mesh):
    placed = (
        P("seq", "head"),
        P("seq", None, "head"),
        P("seq", "head"),
        P("head", "seq"),
        P("head"),
        P("head"),
        P("seq"),
        P(None, "head"),
        P(None, None, "head"),
        P("head"),
        P("head", "seq"),
    )
    return jax.shard_map(
        on_device, mesh=mesh, in_specs=placed, out_specs=P("seq", "head"), check_vma=False
    )
```

profile of v0, /device:TPU:10, one launch (start us, length us, event | category | flops | bytes accessed | tf_op | source)
XLA Modules:
  0.0 453.6 jit_solution(9445835178322954886)
XLA Ops:
  7.4 3.4 collective-permute-start
  11.7 3.4 collective-permute-start.2
  15.9 3.4 collective-permute-start.1
  19.3 1.3 slice.112
  28.5 2.0 slice_compare_fusion.2
  32.5 2.1 multiply_convert_fusion.1
  35.6 1.5 convolution_add_fusion
  39.5 16.1 %all-reduce = f32[256]{0:T(256)S(1)} all-reduce(f32[256]{0:T(256)S(1)} %dynamic-update-slice), channel_id=2, replica_groups=mesh['seq'=8,'head'=4] {'seq'}, use_global_device_ids=true, to_apply=%add | all-reduce | flops 256 | bytes 2048
  56.1 2.3 fusion.1
  58.4 2.8 fusion.23
  61.1 98.9 %all-gather.7.cloned.1.call-done = f32[256,64,128]{2,1,0:T(8,128)} async-done(((f32[32,64,128]{2,1,0:T(8,128)}), f32[256,64,128]{2,1,0:T(8,128)}) %all-gather.7.cloned.1.call-update) | async-done | bytes 8388624 | tf_op jit(solution)/shard_map/all_gather | solution.py:18
  160.1 3.2 while.12
  160.2 1.4 bitcast_add_fusion.2
  161.7 1.4 bitcast_add_fusion.2
  164.9 3.8 fusion.3
  168.7 2.3 copy.59
  171.1 1.9 fusion.19
  173.0 4.0 mul.281
  177.0 2.3 reduce_sum.9
  180.0 2.2 copy.66
  182.2 205.9 %all-gather.5.cloned.1.call-done = bf16[2048,4096]{1,0:T(8,128)(2,1)} async-done(((bf16[2048,512]{1,0:T(8,128)(2,1)}), bf16[2048,4096]{1,0:T(8,128)(2,1)}) %all-gather.5.cloned.1.call-update) | async-done | bytes 16777232 | tf_op jit(solution)/shard_map/all_gather | solution.py:151
  388.0 13.1 %fusion.11 = f32[256,4096]{1,0:T(8,128)} fusion(bf16[2048,4096]{1,0:T(8,128)(2,1)} %all-gather.5.cloned.1.call-done, f32[256,2048]{1,0:T(8,128)} %bitcast.81, f32[2048]{0:T(1024)S(1)} %copy-done.5, f32[256,2048]{1,0:T(8,128)S(1)} %copy.59, bf16[256,2048]{1,0:T(8,128)(2,1)S(1)} %copy-done.2), kind=kOutput, calls=%fused_computation.24 | convolution fusion | flops 4299685888 | bytes 26222592 | tf_op jit(solution)/shard_map/dot_general | solution.py:149
  401.2 43.8 %reduce-scatter.2.cloned.1.call-done = f32[256,1024]{1,0:T(8,128)} async-done(((f32[256,4096]{1,0:T(8,128)}), f32[256,1024]{1,0:T(8,128)}) %reduce-scatter.2.cloned.1.call-update) | async-done | bytes 1048592 | tf_op jit(solution)/shard_map/reduce_scatter | solution.py:154
  445.0 2.1 convert_element_type.84
  (62 shorter events, 16.5 us)
Async XLA Ops:
  6.5 25.9 %copy-start.1 = (bf16[256,2048]{1,0:T(8,128)(2,1)S(1)}, bf16[256,2048]{1,0:T(8,128)(2,1)}, u32[]{:S(2)}) copy-start(bf16[256,2048]{1,0:T(8,128)(2,1)} %param.13) | copy-start | bytes 3145732
  6.5 153.5 %all-gather.7.cloned.1.call-start = ((), (), s32[]{:S(2)}) async-start(), calls=%async_computation.3 | async-start | bytes 9437184 | tf_op jit(solution)/shard_map/all_gather | solution.py:18
  7.4 18.4 %collective-permute-start = (bf16[3]{0:T(256)(128)(2,1)S(1)}, bf16[3]{0:T(256)(128)(2,1)S(1)}, u32[]{:S(2)}, u32[]{:S(2)}) collective-permute-start(bf16[3]{0:T(256)(128)(2,1)S(1)} %slice.86), channel_id=1, source_target_pairs={{0,4},{4,8},{8,12},{12,16},{16,20},{20,24},{24,28},{1,5},{5,9},{9,... | collective-permute-start | bytes 26 | tf_op jit(solution)/shard_map/ppermute | solution.py:32
  11.7 19.9 %collective-permute-start.2 = (bf16[3,2,256]{0,2,1:T(8,128)(2,1)S(1)}, bf16[3,2,256]{0,2,1:T(8,128)(2,1)S(1)}, u32[]{:S(2)}, u32[]{:S(2)}) collective-permute-start(bf16[3,2,256]{0,2,1:T(8,128)(2,1)S(1)} %copy.52), channel_id=1, source_target_pairs={{0,4},{4,8},{8,12},{12,16},{16,20},{20,24},{24,28},{1,5},{5,9},{9,... | collective-permute-start | bytes 9224 | tf_op jit(solution)/shard_map/ppermute | solution.py:32
  15.9 16.6 %collective-permute-start.1 = (bf16[3,2048]{1,0:T(4,128)(2,1)S(1)}, bf16[3,2048]{1,0:T(4,128)(2,1)S(1)}, u32[]{:S(2)}, u32[]{:S(2)}) collective-permute-start(bf16[3,2048]{1,0:T(4,128)(2,1)S(1)} %slice.88), channel_id=1, source_target_pairs={{0,4},{4,8},{8,12},{12,16},{16,20},{20,24},{24,28},{1,5},{5,9},{9,... | collective-permute-start | bytes 36872 | tf_op jit(solution)/shard_map/ppermute | solution.py:32
  37.1 0.8 copy-start.6
  37.1 2.0 copy-start.3
  37.1 350.9 %all-gather.5.cloned.1.call-start = ((), (), s32[]{:S(2)}) async-start(), calls=%async_computation.1 | async-start | bytes 18874368 | tf_op jit(solution)/shard_map/all_gather | solution.py:151
  37.9 407.1 %reduce-scatter.2.cloned.1.call-start = ((), (), s32[]{:S(2)}) async-start(), calls=%async_computation.2 | async-start | bytes 5242880 | tf_op jit(solution)/shard_map/reduce_scatter | solution.py:154
  163.3 1.6 copy-start
  163.3 1.6 copy-start.4
  168.7 2.4 copy-start.2
  180.0 208.1 %copy-start.5 = (f32[2048]{0:T(1024)S(1)}, f32[2048]{0:T(1024)}, u32[]{:S(2)}) copy-start(f32[2048]{0:T(1024)} %param.22) | copy-start | bytes 24580
Sparse Core Ops, SparseCore 0:
  37.3 122.7 all-gather.6
  162.1 225.9 all-gather.4
  401.3 43.6 reduce-scatter.1
where the time goes:
time: 457 us; the launch traced here: 454 us
  waiting for transfers between devices  349 us (76%)
  matrix products  21.3 us (5%)
  other arithmetic  20.6 us (5%)
  local copies, waits for them, and re-layouts  20.3 us (4%)
  blocking collectives  16.1 us (4%)
  between operations  15.3 us (3%)
  starting transfers between devices  10.4 us (2%)
    all_gather x1, waiting for transfers between devices, on_device(): lax.all_gather(output_weight, 'seq', axis=1, tiled=True)  206 us
    all_gather x1, waiting for transfers between devices, entering(): gathered = jax.tree.map(lambda a: lax.all_gather(a, axis), part)  98.9 us
    reduce_scatter x1, waiting for transfers between devices, on_device(): lax.psum_scatter(partial_value, 'head', scatter_dimension=1, tiled=True)  43.8 us
    unnamed x1, blocking collectives  16.1 us
    dot_general x1, matrix products, on_device(): jnp.dot(normed, lax.all_gather(output_weight, 'seq', axis=1, tiled=True),...  13.1 us
    ppermute x3, starting transfers between devices, passed_along(): lax.ppermute(value, axis, [(source, source + steps) for source in range(i...  10.3 us
  transfers between devices with their start and end apart: 6, of which 3 were waited for; matrix products, arithmetic and copies ran while one was open for 9% of the time, Pallas kernels for 0%

commit v1 on v0

--- a/solution.py
+++ b/solution.py
@@ -1,6 +1,8 @@
 import jax
 import jax.numpy as jnp
 from jax import lax
+from jax.experimental import pallas as pl
+from jax.experimental.pallas import tpu as pltpu
 from jax.sharding import PartitionSpec as P
 
 HEAD_DIM = 64
@@ -156,6 +158,510 @@
     )
 
 
+MESH = pl.DeviceIdType.MESH
+SPAN = 256
+CHANNELS = 2048
+HALF = 1024
+HEADS_HERE = 32
+MIB = 1 << 20
+
+
+def scan_kernel(
+    inner_ref,
+    halo_ref,
+    state_ref,
+    step_ref,
+    decay_ref,
+    skip_ref,
+    marks_ref,
+    rows_ref,
+    filter_inner_ref,
+    filter_state_ref,
+    part_ref,
+    infl_ref,
+    dep_ref,
+    read_ref,
+    ext,
+    conv,
+    sconv,
+    weighted,
+):
+    def convolve(source, at, halo_at, taps, target):
+        lanes = pl.ds(at, 256)
+        ext[0:8, :] = halo_ref[:, pl.ds(halo_at, 256)]
+        ext[8:264, :] = source[:, lanes].astype(jnp.float32)
+        running = marks_ref[:, 2:3] * (ext[5:261, :] * taps[0:1, lanes])
+        running = running + marks_ref[:, 1:2] * (ext[6:262, :] * taps[1:2, lanes])
+        running = running + marks_ref[:, 0:1] * (ext[7:263, :] * taps[2:3, lanes])
+        running = running + ext[8:264, :] * taps[3:4, lanes]
+        target[:, lanes] = (running * jax.nn.sigmoid(running)).astype(jnp.bfloat16)
+
+    @pl.loop(0, CHANNELS // 256)
+    def _(i):
+        at = pl.multiple_of(i * 256, 256)
+        convolve(inner_ref, at, at, filter_inner_ref, conv)
+
+    @pl.loop(0, 2)
+    def _(i):
+        at = pl.multiple_of(i * 256, 256)
+        convolve(state_ref, at, pl.multiple_of(at + CHANNELS, 256), filter_state_ref, sconv)
+
+    read_ref[...] = sconv[:, 256:512]
+    value = step_ref[...]
+    step = jnp.maximum(value, 0.0) + jnp.log1p(jnp.exp(-jnp.abs(value)))
+    decay = -step * jnp.exp(decay_ref[...])
+    row_at = lax.broadcasted_iota(jnp.int32, (SPAN, SPAN), 0)
+    col_at = lax.broadcasted_iota(jnp.int32, (SPAN, SPAN), 1)
+    upper = (row_at <= col_at).astype(jnp.float32)
+    cumulative = jnp.dot(
+        decay, upper, precision=highest, preferred_element_type=jnp.float32
+    )
+    documents = rows_ref[0:1, :]
+    inflow = jnp.exp(cumulative) * rows_ref[1:2, :]
+    closing = jnp.exp(cumulative[:, SPAN - 1 :] - cumulative) * rows_ref[2:3, :] * step
+    cum_cols = cumulative.T
+    in_cols = inflow.T
+    close_cols = closing.T
+    linked = (marks_ref[:, 3:4] == documents) & (row_at >= col_at)
+    low = lax.broadcasted_iota(jnp.int32, (SPAN, 128), 1) < HEAD_DIM
+    for group in range(2):
+        lanes = slice(group * 128, group * 128 + 128)
+        writes = sconv[:, lanes]
+        scores = lax.dot_general(
+            sconv[:, 256 + group * 128 : 384 + group * 128],
+            writes,
+            (((1,), (1,)), ((), ())),
+            preferred_element_type=jnp.float32,
+        )
+        scores = jnp.where(linked, scores, 0.0)
+        for pair in range(8):
+            first = group * 16 + pair * 2
+            at = slice(first * HEAD_DIM, first * HEAD_DIM + 128)
+            x = conv[:, at]
+
+            def mixed(h):
+                spread = jnp.minimum(cum_cols[:, h : h + 1] - cumulative[h : h + 1, :], 0.0)
+                mixing = (jnp.exp(spread) * scores * step[h : h + 1, :]).astype(jnp.bfloat16)
+                return jnp.dot(mixing, x, preferred_element_type=jnp.float32)
+
+            def both(cols):
+                return jnp.where(low, cols[:, first : first + 1], cols[:, first + 1 : first + 2])
+
+            x32 = x.astype(jnp.float32)
+            gain = jnp.where(low, skip_ref[first], skip_ref[first + 1])
+            part_ref[:, at] = jnp.where(low, mixed(first), mixed(first + 1)) + gain * x32
+            weighted[:, at] = (x32 * both(close_cols)).astype(jnp.bfloat16)
+            infl_ref[:, at] = both(in_cols)
+        wide = slice(group * HALF, group * HALF + HALF)
+        dep_ref[:, wide] = lax.dot_general(
+            writes,
+            weighted[:, wide],
+            (((0,), (0,)), ((), ())),
+            preferred_element_type=jnp.float32,
+        )
+
+
+def mix_kernel(
+    part_ref,
+    infl_ref,
+    dep_ref,
+    read_ref,
+    gate_ref,
+    gain_ref,
+    weight_ref,
+    out_ref,
+    weight_in,
+    dep_stage,
+    dep_in,
+    fade_stage,
+    fade_in,
+    chain_out,
+    chain_in,
+    state_out,
+    state_in,
+    state_own,
+    acts,
+    partial,
+    partial_own,
+    sums_in,
+    final_out,
+    final_in,
+    weight_sems,
+    pair_sems,
+    chain_sems,
+    state_sems,
+    act_send,
+    act_recv,
+    sum_send,
+    sum_recv,
+    final_send,
+    final_recv,
+):
+    s = lax.axis_index("seq")
+    h = lax.axis_index("head")
+    z, y = s // 2, s % 2
+    me = s * 4 + h
+    z_near = z + 1 - 2 * (z % 2)
+    z_far = (z + 2) % 4
+
+    def remote(src, dst, send, recv, seq, head=h):
+        return pltpu.make_async_remote_copy(
+            src_ref=src,
+            dst_ref=dst,
+            send_sem=send,
+            recv_sem=recv,
+            device_id=(seq, head),
+            device_id_type=MESH,
+        )
+
+    barrier = pltpu.get_barrier_semaphore()
+
+    @pl.loop(1, 32)
+    def _(i):
+        other = lax.rem(me + i, 32)
+        pl.semaphore_signal(
+            barrier, inc=1, device_id=(other // 4, other % 4), device_id_type=MESH
+        )
+
+    pl.semaphore_wait(barrier, 31)
+
+    y_pair = 2 * z + 1 - y
+    own = pl.ds(pl.multiple_of(y * HALF, HALF), HALF)
+    apart = pl.ds(pl.multiple_of((1 - y) * HALF, HALF), HALF)
+
+    dep_stage[...] = dep_ref[:, apart].astype(jnp.bfloat16)
+    fade_stage[...] = infl_ref[SPAN - 8 : SPAN, apart]
+    send_dep = remote(dep_stage, dep_in, pair_sems.at[0], pair_sems.at[1], y_pair)
+    send_fade = remote(fade_stage, fade_in, pair_sems.at[2], pair_sems.at[3], y_pair)
+    send_fade.start()
+    send_dep.start()
+    send_weight = remote(
+        weight_ref, weight_in, weight_sems.at[0], weight_sems.at[1], 2 * z_near + y
+    )
+    send_weight.start()
+
+    @pl.when(z == 0)
+    def _():
+        chain_in[...] = jnp.zeros_like(chain_in)
+
+    send_fade.wait_recv()
+    send_dep.wait_recv()
+    is_first = y == 0
+    chain_copies = [
+        remote(
+            chain_out.at[q],
+            chain_in.at[q],
+            chain_sems.at[0, q],
+            chain_sems.at[1, q],
+            jnp.minimum(s + 2, 7),
+        )
+        for q in range(4)
+    ]
+    state_copies = [
+        remote(state_out.at[q], state_in.at[q], state_sems.at[0, q], state_sems.at[1, q], y_pair)
+        for q in range(4)
+    ]
+    for q in range(4):
+        lanes = pl.ds(pl.multiple_of(y * HALF + q * 256, 256), 256)
+        here = slice(q * 256, q * 256 + 256)
+        dep_own = dep_ref[:, lanes]
+        dep_other = dep_in[:, here].astype(jnp.float32)
+        fade_own = infl_ref[SPAN - 1 : SPAN, lanes]
+        fade_other = fade_in[7:8, here]
+        dep_0 = jnp.where(is_first, dep_own, dep_other)
+        dep_1 = jnp.where(is_first, dep_other, dep_own)
+        fade_0 = jnp.where(is_first, fade_own, fade_other)
+        fade_1 = jnp.where(is_first, fade_other, fade_own)
+        slab = fade_1 * dep_0 + dep_1
+        slab_fade = fade_0 * fade_1
+
+        @pl.when(z > 0)
+        def _():
+            chain_copies[q].wait_recv()
+
+        entering_0 = chain_in[q].astype(jnp.float32)
+        chain_out[q] = (slab_fade * entering_0 + slab).astype(jnp.bfloat16)
+
+        @pl.when(z < 3)
+        def _():
+            chain_copies[q].start()
+
+        entering_1 = fade_0 * entering_0 + dep_0
+        state_own[:, here] = jnp.where(is_first, entering_0, entering_1).astype(jnp.bfloat16)
+        state_out[q] = jnp.where(is_first, entering_1, entering_0).astype(jnp.bfloat16)
+        state_copies[q].start()
+
+    def norm_half(half, state):
+        lanes = pl.ds(pl.multiple_of(half * HALF, HALF), HALF)
+        reads_at = pl.ds(pl.multiple_of(half * 128, 128), 128)
+
+        @pl.loop(0, 4)
+        def _(i):
+            rows = pl.ds(pl.multiple_of(i * 64, 64), 64)
+            read = jnp.dot(read_ref[rows, reads_at], state, preferred_element_type=jnp.float32)
+            gate = gate_ref[rows, lanes].astype(jnp.float32)
+            scan = part_ref[rows, lanes] + infl_ref[rows, lanes] * read
+            gated = scan * (gate * jax.nn.sigmoid(gate))
+            mean = jnp.sum(gated * gated, axis=1, keepdims=True) * (1.0 / HALF)
+            normed = gated * lax.rsqrt(mean + 1e-05) * gain_ref[:, lanes]
+            acts[0, half, rows, :] = normed.astype(jnp.bfloat16)
+
+    def send_act(slot, half, source, seq):
+        return remote(
+            acts.at[source, half],
+            acts.at[slot, half],
+            act_send.at[slot - 1, half],
+            act_recv.at[slot - 1, half],
+            seq,
+        )
+
+    z_pair = 2 * z_far + y
+    norm_half(y, state_own[...])
+    send_act(2, y, 0, z_pair).start()
+    send_act(1, y, 0, y_pair).start()
+    for q in range(4):
+        state_copies[q].wait_recv()
+    norm_half(1 - y, jnp.concatenate([state_in[q] for q in range(4)], axis=1))
+    send_act(2, 1 - y, 0, z_pair).start()
+    send_act(1, 1 - y, 0, y_pair).start()
+
+    def sum_copy(k, o):
+        to = h ^ o
+        rows = pl.ds(pl.multiple_of(to * 64, 64), 64)
+        return remote(
+            partial.at[k, rows],
+            sums_in.at[k, o - 1],
+            sum_send.at[k, o - 1],
+            sum_recv.at[k, o - 1],
+            s,
+            to,
+        )
+
+    def project(k):
+        for side, weight in enumerate((weight_ref, weight_in)):
+
+            @pl.loop(0, 2)
+            def _(i):
+                lanes = pl.ds(pl.multiple_of(i * 256, 256), 256)
+                spot = pl.ds(pl.multiple_of(side * 512 + i * 256, 256), 256)
+                total = jnp.dot(
+                    acts[k, 0], weight[0:HALF, lanes], preferred_element_type=jnp.float32
+                ) + jnp.dot(
+                    acts[k, 1], weight[HALF:CHANNELS, lanes], preferred_element_type=jnp.float32
+                )
+                partial_own[k, :, spot] = total
+                partial[k, :, spot] = total.astype(jnp.bfloat16)
+
+        for o in (2, 3, 1):
+            sum_copy(k, o).start()
+
+    def final_parts(k):
+        zt = z if k < 2 else z_far
+        yt = y if k % 2 == 0 else 1 - y
+        rows = pl.ds(pl.multiple_of(h * 64, 64), 64)
+        spot = pl.ds(pl.multiple_of(y * 512, 512), 512)
+        parts = []
+        for side, head in enumerate((z, z_near)):
+            target = 2 * zt + yt
+            stays = (target == s) & (head == h)
+            copy = remote(
+                final_out.at[k, side],
+                final_in.at[rows, spot],
+                final_send.at[k, side],
+                final_recv.at[y * 4 + h],
+                target,
+                head,
+            )
+            parts.append((side, stays, copy))
+        return rows, spot, parts
+
+    def finish(k):
+        for o in (1, 2, 3):
+            sum_copy(k, o).wait_recv()
+        rows, spot, parts = final_parts(k)
+        total = partial_own[k, rows, :]
+        for o in range(3):
+            total = total + sums_in[k, o].astype(jnp.float32)
+        total = total.astype(jnp.bfloat16)
+        for side, stays, copy in parts:
+            final_out[k, side] = total[:, side * 512 : side * 512 + 512]
+
+            @pl.when(stays)
+            def _():
+                final_in[rows, spot] = total[:, side * 512 : side * 512 + 512]
+
+            @pl.when(jnp.logical_not(stays))
+            def _():
+                copy.start()
+
+    send_weight.wait_recv()
+    project(0)
+    send_act(1, 1 - y, 0, y_pair).wait_recv()
+    send_act(1, y, 0, y_pair).wait_recv()
+    project(1)
+    for half in (y, 1 - y):
+        send_act(2, half, 0, z_pair).wait_recv()
+        send_act(3, half, 2, y_pair).start()
+    finish(0)
+    project(2)
+    finish(1)
+    send_act(3, 1 - y, 2, y_pair).wait_recv()
+    send_act(3, y, 2, y_pair).wait_recv()
+    project(3)
+    finish(2)
+    finish(3)
+
+    z_from = 2 * (h // 2) + z % 2
+    for y_from in range(2):
+        for h_from in range(4):
+            rows = slice(h_from * 64, h_from * 64 + 64)
+            spot = slice(y_from * 512, y_from * 512 + 512)
+            mine = (z_from == z) & (y_from == y) & (h_from == h)
+
+            @pl.when(jnp.logical_not(mine))
+            def _():
+                remote(
+                    final_out.at[0, 0],
+                    final_in.at[rows, spot],
+                    final_send.at[0, 0],
+                    final_recv.at[y_from * 4 + h_from],
+                    2 * z_from + y_from,
+                    h_from,
+                ).wait_recv()
+
+    out_ref[...] = final_in[...]
+
+    send_dep.wait_send()
+    send_fade.wait_send()
+    send_weight.wait_send()
+    for q in range(4):
+        state_copies[q].wait_send()
+
+        @pl.when(z < 3)
+        def _():
+            chain_copies[q].wait_send()
+
+    for half in range(2):
+        send_act(1, half, 0, y_pair).wait_send()
+        send_act(2, half, 0, z_pair).wait_send()
+        send_act(3, half, 2, y_pair).wait_send()
+    for k in range(4):
+        for o in (1, 2, 3):
+            sum_copy(k, o).wait_send()
+        for side, stays, copy in final_parts(k)[2]:
+
+            @pl.when(jnp.logical_not(stays))
+            def _():
+                copy.wait_send()
+
+
+def on_device_fast(
+    inner_input,
+    state_input,
+    gate_input,
+    step_input,
+    decay_exponent,
+    skip_gain,
+    documents,
+    filter_inner,
+    filter_state,
+    norm_gain,
+    output_weight,
+):
+    margin = KERNEL - 1
+    state_flat = state_input.reshape(SPAN, 512)
+    edge = jnp.concatenate(
+        [
+            inner_input[-margin:],
+            state_flat[-margin:],
+            jnp.broadcast_to(documents[-margin:, None].astype(jnp.bfloat16), (margin, 128)),
+        ],
+        axis=1,
+    )
+    before = passed_along(edge, "seq", 1).astype(jnp.float32)
+    halo = jnp.pad(before, ((8 - margin, 0), (0, 0)))
+    docs = documents.astype(jnp.float32)
+    wide = jnp.concatenate([before[:, CHANNELS + 512], docs])
+    marks = [(wide[margin - k : margin - k + SPAN] == docs).astype(jnp.float32) for k in (1, 2, 3)]
+    marks = jnp.stack(marks + [docs] * 5, axis=1)
+    rows = jnp.stack(
+        [docs, (docs == wide[margin - 1]).astype(jnp.float32)]
+        + [(docs == docs[-1]).astype(jnp.float32)] * 6
+    )
+    vmem = pl.BlockSpec(memory_space=pltpu.VMEM)
+    smem = pl.BlockSpec(memory_space=pltpu.SMEM)
+    part, infl, dep, reads = pl.pallas_call(
+        scan_kernel,
+        out_shape=(
+            jax.ShapeDtypeStruct((SPAN, CHANNELS), jnp.float32),
+            jax.ShapeDtypeStruct((SPAN, CHANNELS), jnp.float32),
+            jax.ShapeDtypeStruct((STATE, CHANNELS), jnp.float32),
+            jax.ShapeDtypeStruct((SPAN, 256), jnp.bfloat16),
+        ),
+        in_specs=[vmem] * 5 + [smem] + [vmem] * 4,
+        out_specs=(vmem,) * 4,
+        scratch_shapes=[
+            pltpu.VMEM((SPAN + 8, 256), jnp.float32),
+            pltpu.VMEM((SPAN, CHANNELS), jnp.bfloat16),
+            pltpu.VMEM((SPAN, 512), jnp.bfloat16),
+            pltpu.VMEM((SPAN, CHANNELS), jnp.bfloat16),
+        ],
+        compiler_params=pltpu.CompilerParams(vmem_limit_bytes=48 * MIB),
+        name="scan_local",
+    )(
+        inner_input,
+        halo,
+        state_flat,
+        step_input,
+        decay_exponent[:, None],
+        skip_gain,
+        marks,
+        rows,
+        filter_inner,
+        filter_state.reshape(KERNEL, 512),
+    )
+    bf16, f32 = jnp.bfloat16, jnp.float32
+    dma = pltpu.SemaphoreType.DMA
+    return pl.pallas_call(
+        mix_kernel,
+        out_shape=jax.ShapeDtypeStruct((SPAN, 1024), bf16),
+        in_specs=[vmem] * 7,
+        out_specs=vmem,
+        scratch_shapes=[
+            pltpu.VMEM((CHANNELS, 512), bf16),
+            pltpu.VMEM((STATE, HALF), bf16),
+            pltpu.VMEM((STATE, HALF), bf16),
+            pltpu.VMEM((8, HALF), f32),
+            pltpu.VMEM((8, HALF), f32),
+            pltpu.VMEM((4, STATE, 256), bf16),
+            pltpu.VMEM((4, STATE, 256), bf16),
+            pltpu.VMEM((4, STATE, 256), bf16),
+            pltpu.VMEM((4, STATE, 256), bf16),
+            pltpu.VMEM((STATE, HALF), bf16),
+            pltpu.VMEM((4, 2, SPAN, HALF), bf16),
+            pltpu.VMEM((4, SPAN, 1024), bf16),
+            pltpu.VMEM((4, SPAN, 1024), f32),
+            pltpu.VMEM((4, 3, 64, 1024), bf16),
+            pltpu.VMEM((4, 2, 64, 512), bf16),
+            pltpu.VMEM((SPAN, 1024), bf16),
+            dma((2,)),
+            dma((4,)),
+            dma((2, 4)),
+            dma((2, 4)),
+            dma((3, 2)),
+            dma((3, 2)),
+            dma((4, 3)),
+            dma((4, 3)),
+            dma((4, 2)),
+            dma((8,)),
+        ],
+        compiler_params=pltpu.CompilerParams(
+            vmem_limit_bytes=56 * MIB, collective_id=0, has_side_effects=True
+        ),
+        name="mix_exchange",
+    )(part, infl, dep, reads, gate_input, norm_gain[None, :], output_weight)
+
+
 def solution(mesh):
     placed = (
         P("seq", "head"),
@@ -170,6 +676,8 @@
         P("head"),
         P("head", "seq"),
     )
+    ways = dict(mesh.shape)
+    fast = ways["seq"] == 8 and ways["head"] == 4
     return jax.shard_map(
-        on_device, mesh=mesh, in_specs=placed, out_specs=P("seq", "head"), check_vma=False
-    )
+        on_device_fast if fast else on_device, mesh=mesh, in_specs=placed, out_specs=P("seq", "head"), check_vma=False
+    )

time: 457 us -> 213 us (0.47)
  waiting for transfers between devices: 349 us -> 0.15 us
  Pallas kernels: 0 us -> 192 us
  matrix products: 21.3 us -> 0 us
  other arithmetic: 20.6 us -> 2.93 us
  blocking collectives: 16.1 us -> 0 us
  between operations: 15.3 us -> 0.07 us
  starting transfers between devices: 10.4 us -> 3.43 us
  local copies, waits for them, and re-layouts: 20.3 us -> 13.7 us
    all_gather x2 -> x0, waiting for transfers between devices: 305 us -> none  [the longest x1 206 us: on_device(): lax.all_gather(output_weight, 'seq', axis=1, tiled=True)]
    pallas_call x0 -> x2, Pallas kernels: none -> 192 us  [the longest x1 184 us: on_device_fast(): pl.pallas_call(mix_kernel, out_shape=jax.ShapeDtypeStruct((SPAN, 1024), b...]
    reduce_scatter x1 -> x0, waiting for transfers between devices: 43.8 us -> none  [on_device(): lax.psum_scatter(partial_value, 'head', scatter_dimension=1, tiled=True)]
    dot_general x5 -> x0, matrix products: 21.3 us -> none  [the longest x1 13.1 us: on_device(): jnp.dot(normed, lax.all_gather(output_weight, 'seq', axis=1, tiled=True),...]
    unnamed x1 -> x0, blocking collectives: 16.1 us -> none
    ppermute x3 -> x1, starting transfers between devices: 10.3 us -> 3.43 us  [passed_along(): lax.ppermute(value, axis, [(source, source + steps) for source in range(i...]
    convert_element_type x5 -> x2, other arithmetic: 7.29 us -> 0.76 us  [the longest x1 0.76 us: on_device_fast(): docs = documents.astype(jnp.float32)]
    mul x5 -> x0, local copies, waits for them, and re-layouts: 5.39 us -> none  [the longest x1 4.03 us: gated_norm(): mean_square = jnp.mean(grouped * grouped, axis=-1, keepdims=True)]
  transfers between devices with their start and end apart: 6 -> 1, of which waited for: 3 -> 1; matrix products, arithmetic and copies ran while one was open for 9% -> 1% of each run, Pallas kernels for 0% -> 0%
where the time goes in v1:
time: 213 us; the launch traced here: 212 us
  Pallas kernels  192 us (90%)
  local copies, waits for them, and re-layouts  13.7 us (6%)
  starting transfers between devices  3.43 us (2%)
  other arithmetic  2.93 us (1%)
    pallas_call x1, Pallas kernels, on_device_fast(): pl.pallas_call(mix_kernel, out_shape=jax.ShapeDtypeStruct((SPAN, 1024), b...  184 us
    unnamed x19, local copies, waits for them, and re-layouts  10.6 us
    pallas_call x1, Pallas kernels, on_device_fast(): pl.pallas_call(scan_kernel, out_shape=(jax.ShapeDtypeStruct((SPAN, CHANNE...  8.45 us
  transfers between devices with their start and end apart: 1, of which 1 were waited for; matrix products, arithmetic and copies ran while one was open for 1% of the time, Pallas kernels for 0%

profile of v1, /device:TPU:10, one launch (start us, length us, event | category | flops | bytes accessed | tf_op | source)
XLA Modules:
  0.0 212.5 jit_solution(10833057691636230746)
XLA Ops:
  0.0 0.8 fusion
  0.8 0.7 slice_bitcast_fusion
  1.5 0.8 slice.33
  2.4 3.4 %collective-permute-start = (bf16[3,2688]{1,0:T(4,128)(2,1)S(1)}, bf16[3,2688]{1,0:T(4,128)(2,1)S(1)}, u32[]{:S(2)}, u32[]{:S(2)}) collective-permute-start(bf16[3,2688]{1,0:T(4,128)(2,1)S(1)} %pad_maximum_fusion), channel_id=1, source_target_pairs={{0,4},{4,8},{8,12},{12,16},{16,20},{20,24},{24,28},{1,5},{5,9},{9,... | collective-permute-start | bytes 48392 | tf_op jit(solution)/shard_map/ppermute | solution.py:34
  5.8 0.6 slice.42
  6.4 0.7 copy.26
  7.1 0.7 copy.22.decay_ref
  7.8 1.0 copy.25
  8.8 0.1 collective-permute-done
  9.0 0.1 slice_reduce_fusion
  9.1 0.1 pad_maximum_fusion.1
  9.2 0.6 slice.44
  9.8 2.1 compare_convert_fusion.2
  11.9 0.1 copy.23.marks_ref
  12.1 1.2 copy-done.1
  13.3 0.8 copy-done.4
  14.1 0.8 copy-done.5
  14.8 0.7 copy-done.6
  15.5 8.5 %scan_local.1 = (f32[256,2048]{1,0:T(8,128)S(1)}, f32[256,2048]{1,0:T(8,128)}, f32[128,2048]{1,0:T(8,128)S(1)}, bf16[256,256]{1,0:T(8,128)(2,1)S(1)}) custom-call(bf16[256,2048]{1,0:T(8,128)(2,1)S(1)} %copy-done.1, f32[8,2688]{1,0:T(8,128)S(1)} %pad.4.halo_ref, bf16[256,512]{1,0:T(8,128)(2,1)S(1)} %bitcast.18, f32[32,256]{1,0:T(8,128)S(1)} %copy-done.4, ...), custom_call_target="tpu_custom_call" | custom-call | tf_op jit(solution)/shard_map/scan_local/pallas_call | solution.py:593
  23.9 1.3 copy-done
  25.2 1.0 copy-done.2
  26.2 0.7 copy-done.3
  26.8 183.8 %mix_exchange.1 = bf16[256,1024]{1,0:T(8,128)(2,1)} custom-call(f32[256,2048]{1,0:T(8,128)} %copy-done, f32[256,2048]{1,0:T(8,128)} %get-tuple-element.10.infl_ref, f32[128,2048]{1,0:T(8,128)} %copy-done.2, bf16[256,256]{1,0:T(8,128)(2,1)} %copy-done.3, bf16[256,2048]{1,0:T(8,128)(2,1)} %gate_ref.1, f32[1,2048]{1,0:T(1,128)} %bitcast.34, ...), custom_call_target="tpu_custom_call" | custom-call | tf_op jit(solution)/shard_map/mix_exchange/pallas_call | solution.py:625
  210.6 1.9 copy.28
  (15 shorter events, 0.3 us)
Async XLA Ops:
  2.4 6.6 %collective-permute-start = (bf16[3,2688]{1,0:T(4,128)(2,1)S(1)}, bf16[3,2688]{1,0:T(4,128)(2,1)S(1)}, u32[]{:S(2)}, u32[]{:S(2)}) collective-permute-start(bf16[3,2688]{1,0:T(4,128)(2,1)S(1)} %pad_maximum_fusion), channel_id=1, source_target_pairs={{0,4},{4,8},{8,12},{12,16},{16,20},{20,24},{24,28},{1,5},{5,9},{9,... | collective-permute-start | bytes 48392 | tf_op jit(solution)/shard_map/ppermute | solution.py:34
  12.1 1.2 copy-start.1
  13.3 0.8 copy-start.4
  14.1 0.8 copy-start.5
  14.8 0.7 copy-start.6
  23.9 1.3 copy-start
  25.2 1.0 copy-start.2
  26.2 0.7 copy-start.3

commit v2 on v0

--- a/solution.py
+++ b/solution.py
@@ -1,6 +1,8 @@
 import jax
 import jax.numpy as jnp
 from jax import lax
+from jax.experimental import pallas as pl
+from jax.experimental.pallas import tpu as pltpu
 from jax.sharding import PartitionSpec as P
 
 HEAD_DIM = 64
@@ -156,6 +158,592 @@
     )
 
 
+MESH = pl.DeviceIdType.MESH
+SPAN = 256
+CHANNELS = 2048
+HALF = 1024
+MIB = 1 << 20
+
+
+def fused_kernel(
+    inner_ref,
+    state_ref,
+    step_ref,
+    decay_ref,
+    documents_ref,
+    filter_inner_ref,
+    filter_state_ref,
+    gain_ref,
+    skip_ref,
+    gate_hbm,
+    weight_hbm,
+    out_ref,
+    gate_ref,
+    weight_ref,
+    weight_in,
+    halo_inner,
+    halo_state,
+    halo_documents,
+    ext,
+    conv,
+    sconv,
+    cum_rows,
+    step_rows,
+    in_rows,
+    close_rows,
+    weighted,
+    part_ref,
+    infl_ref,
+    dep_ref,
+    dep_stage,
+    dep_in,
+    fade_stage,
+    fade_in,
+    chain_out,
+    chain_in,
+    state_out,
+    state_in,
+    state_own,
+    acts,
+    partial,
+    partial_own,
+    sums_in,
+    final_out,
+    final_in,
+    local_sems,
+    halo_sems,
+    weight_sems,
+    pair_sems,
+    chain_sems,
+    state_sems,
+    act_send,
+    act_recv,
+    sum_send,
+    sum_recv,
+    final_send,
+    final_recv,
+):
+    s = lax.axis_index("seq")
+    h = lax.axis_index("head")
+    z, y = s // 2, s % 2
+    me = s * 4 + h
+    z_near = z + 1 - 2 * (z % 2)
+    z_far = (z + 2) % 4
+    y_pair = 2 * z + 1 - y
+    z_pair = 2 * z_far + y
+
+    def remote(src, dst, send, recv, seq, head=h):
+        return pltpu.make_async_remote_copy(
+            src_ref=src,
+            dst_ref=dst,
+            send_sem=send,
+            recv_sem=recv,
+            device_id=(seq, head),
+            device_id_type=MESH,
+        )
+
+    gate_copy = pltpu.make_async_copy(gate_hbm, gate_ref, local_sems.at[0])
+    weight_copy = pltpu.make_async_copy(weight_hbm, weight_ref, local_sems.at[1])
+    gate_copy.start()
+    weight_copy.start()
+
+    barrier = pltpu.get_barrier_semaphore()
+
+    @pl.loop(1, 32)
+    def _(i):
+        other = lax.rem(me + i, 32)
+        pl.semaphore_signal(
+            barrier, inc=1, device_id=(other // 4, other % 4), device_id_type=MESH
+        )
+
+    pl.semaphore_wait(barrier, 31)
+
+    after = jnp.minimum(s + 1, 7)
+    halo_copies = [
+        remote(source, target, halo_sems.at[0, i], halo_sems.at[1, i], after)
+        for i, (source, target) in enumerate(
+            (
+                (documents_ref, halo_documents),
+                (state_ref.at[pl.ds(SPAN - 16, 16)], halo_state),
+                (inner_ref.at[pl.ds(SPAN - 16, 16)], halo_inner),
+            )
+        )
+    ]
+
+    @pl.when(s < 7)
+    def _():
+        for copy in halo_copies:
+            copy.start()
+
+    weight_copies = []
+    for i in range(4):
+        rows = pl.ds(i * 512, 512)
+        weight_copies.append(
+            remote(
+                weight_hbm.at[rows],
+                weight_in.at[rows],
+                weight_sems.at[0, i],
+                weight_sems.at[1, i],
+                2 * z_near + y,
+            )
+        )
+    weight_copies[0].start()
+
+    @pl.when(z % 2 == 1)
+    def _():
+        for copy in weight_copies[1:]:
+            copy.start()
+
+    @pl.when(s == 0)
+    def _():
+        halo_documents[...] = jnp.zeros_like(halo_documents)
+        halo_state[...] = jnp.zeros_like(halo_state)
+        halo_inner[...] = jnp.zeros_like(halo_inner)
+
+    diagonal = lax.broadcasted_iota(jnp.int32, (32, 32), 0) == lax.broadcasted_iota(
+        jnp.int32, (32, 32), 1
+    )
+    rate = jnp.sum(
+        jnp.where(diagonal, jnp.broadcast_to(jnp.exp(decay_ref[...]), (32, 32)), 0.0),
+        axis=1,
+        keepdims=True,
+    )
+    value = step_ref[...]
+    step = jnp.maximum(value, 0.0) + jnp.log1p(jnp.exp(-jnp.abs(value)))
+    row_at = lax.broadcasted_iota(jnp.int32, (SPAN, SPAN), 0)
+    col_at = lax.broadcasted_iota(jnp.int32, (SPAN, SPAN), 1)
+    upper = (row_at <= col_at).astype(jnp.float32)
+    cumulative = jnp.dot(
+        -step * rate, upper, precision=highest, preferred_element_type=jnp.float32
+    )
+    documents = documents_ref[...].astype(jnp.float32)
+    final = (documents == documents[:, SPAN - 1 :]).astype(jnp.float32)
+    step_rows[...] = step
+    cum_rows[...] = cumulative
+    close_rows[...] = jnp.exp(cumulative[:, SPAN - 1 :] - cumulative) * final * step
+
+    @pl.when(s > 0)
+    def _():
+        for copy in halo_copies:
+            copy.wait_recv()
+
+    before = halo_documents[...].astype(jnp.float32)
+    in_rows[...] = jnp.exp(cumulative) * (documents == before[:, SPAN - 1 :]).astype(jnp.float32)
+    lane = lax.broadcasted_iota(jnp.int32, (8, SPAN), 1)
+    mark_row = lax.broadcasted_iota(jnp.int32, (8, SPAN), 0)
+    documents_8 = jnp.broadcast_to(documents, (8, SPAN))
+    before_8 = jnp.broadcast_to(before, (8, SPAN))
+    mark_rows = documents_8
+    for k in (1, 2, 3):
+        shifted = jnp.where(
+            lane < k, pltpu.roll(before_8, k, axis=1), pltpu.roll(documents_8, k, axis=1)
+        )
+        same = (shifted == documents_8).astype(jnp.float32)
+        mark_rows = jnp.where(mark_row == k, same, mark_rows)
+    marks = mark_rows.T
+
+    def convolve(source, halo, at, taps, target):
+        lanes = pl.ds(at, 256)
+        ext[0:16, :] = halo[:, lanes].astype(jnp.float32)
+        ext[16:272, :] = source[:, lanes].astype(jnp.float32)
+        running = marks[:, 3:4] * (ext[13:269, :] * taps[0:1, lanes])
+        running = running + marks[:, 2:3] * (ext[14:270, :] * taps[1:2, lanes])
+        running = running + marks[:, 1:2] * (ext[15:271, :] * taps[2:3, lanes])
+        running = running + ext[16:272, :] * taps[3:4, lanes]
+        target[:, lanes] = (running * jax.nn.sigmoid(running)).astype(jnp.bfloat16)
+
+    @pl.loop(0, 2)
+    def _(i):
+        convolve(state_ref, halo_state, pl.multiple_of(i * 256, 256), filter_state_ref, sconv)
+
+    linked = (marks[:, 0:1] == documents) & (row_at >= col_at)
+    low = lax.broadcasted_iota(jnp.int32, (SPAN, 128), 1) < HEAD_DIM
+
+    apart = pl.ds(pl.multiple_of((1 - y) * HALF, HALF), HALF)
+    send_dep = remote(dep_stage, dep_in, pair_sems.at[0], pair_sems.at[1], y_pair)
+    send_fade = remote(fade_stage, fade_in, pair_sems.at[2], pair_sems.at[3], y_pair)
+
+    @pl.loop(0, 2)
+    def _(turn):
+        group = jnp.where(turn == 0, 1 - y, y)
+        base = group * HALF
+
+        @pl.loop(0, 4)
+        def _(i):
+            at = pl.multiple_of(base + i * 256, 256)
+            convolve(inner_ref, halo_inner, at, filter_inner_ref, conv)
+
+        writes = sconv[:, pl.ds(pl.multiple_of(group * 128, 128), 128)]
+        reads = sconv[:, pl.ds(pl.multiple_of(256 + group * 128, 128), 128)]
+        scores = lax.dot_general(
+            reads, writes, (((1,), (1,)), ((), ())), preferred_element_type=jnp.float32
+        )
+        scores = jnp.where(linked, scores, 0.0)
+        heads = pl.ds(pl.multiple_of(group * 16, 16), 16)
+        cums = cum_rows[heads, :]
+        steps = step_rows[heads, :]
+        cum_cols = cums.T
+        in_cols = in_rows[heads, :].T
+        close_cols = close_rows[heads, :].T
+        for pair in range(8):
+            first = pair * 2
+            at = pl.ds(pl.multiple_of(base + pair * 128, 128), 128)
+            x = conv[:, at]
+
+            def mixed(j):
+                spread = jnp.minimum(cum_cols[:, j : j + 1] - cums[j : j + 1, :], 0.0)
+                mixing = (jnp.exp(spread) * scores * steps[j : j + 1, :]).astype(jnp.bfloat16)
+                return jnp.dot(mixing, x, preferred_element_type=jnp.float32)
+
+            def both(cols):
+                return jnp.where(low, cols[:, first : first + 1], cols[:, first + 1 : first + 2])
+
+            x32 = x.astype(jnp.float32)
+            gain = jnp.where(low, skip_ref[group * 16 + first], skip_ref[group * 16 + first + 1])
+            part_ref[:, at] = jnp.where(low, mixed(first), mixed(first + 1)) + gain * x32
+            weighted[:, pair * 128 : pair * 128 + 128] = (x32 * both(close_cols)).astype(
+                jnp.bfloat16
+            )
+            infl_ref[:, at] = both(in_cols)
+        dep_ref[...] = lax.dot_general(
+            writes, weighted[...], (((0,), (0,)), ((), ())), preferred_element_type=jnp.float32
+        )
+
+        @pl.when(turn == 0)
+        def _():
+            dep_stage[...] = dep_ref[...].astype(jnp.bfloat16)
+            fade_stage[...] = infl_ref[SPAN - 8 : SPAN, apart]
+            send_fade.start()
+            send_dep.start()
+
+    @pl.when(z == 0)
+    def _():
+        chain_in[...] = jnp.zeros_like(chain_in)
+
+    send_fade.wait_recv()
+    send_dep.wait_recv()
+    is_first = y == 0
+    chain_copies = [
+        remote(
+            chain_out.at[q],
+            chain_in.at[q],
+            chain_sems.at[0, q],
+            chain_sems.at[1, q],
+            jnp.minimum(s + 2, 7),
+        )
+        for q in range(4)
+    ]
+    state_copies = [
+        remote(state_out.at[q], state_in.at[q], state_sems.at[0, q], state_sems.at[1, q], y_pair)
+        for q in range(4)
+    ]
+    for q in range(4):
+        lanes = pl.ds(pl.multiple_of(y * HALF + q * 256, 256), 256)
+        here = slice(q * 256, q * 256 + 256)
+        dep_own = dep_ref[:, here]
+        dep_other = dep_in[:, here].astype(jnp.float32)
+        fade_own = infl_ref[SPAN - 8 : SPAN, lanes][7:8]
+        fade_other = fade_in[7:8, here]
+        dep_0 = jnp.where(is_first, dep_own, dep_other)
+        dep_1 = jnp.where(is_first, dep_other, dep_own)
+        fade_0 = jnp.where(is_first, fade_own, fade_other)
+        fade_1 = jnp.where(is_first, fade_other, fade_own)
+        slab = fade_1 * dep_0 + dep_1
+        slab_fade = fade_0 * fade_1
+
+        @pl.when(z > 0)
+        def _():
+            chain_copies[q].wait_recv()
+
+        entering_0 = chain_in[q].astype(jnp.float32)
+        chain_out[q] = (slab_fade * entering_0 + slab).astype(jnp.bfloat16)
+
+        @pl.when(z < 3)
+        def _():
+            chain_copies[q].start()
+
+        entering_1 = fade_0 * entering_0 + dep_0
+        state_own[:, here] = jnp.where(is_first, entering_0, entering_1).astype(jnp.bfloat16)
+        state_out[q] = jnp.where(is_first, entering_1, entering_0).astype(jnp.bfloat16)
+        state_copies[q].start()
+
+    @pl.when(z % 2 == 0)
+    def _():
+        for copy in weight_copies[1:]:
+            copy.start()
+
+    gate_copy.wait()
+
+    def act_copy(slot, half, quarter):
+        source = 2 if slot == 3 else 0
+        rows = pl.ds(quarter * 128, 128)
+        return remote(
+            acts.at[source, half, rows],
+            acts.at[slot, half, rows],
+            act_send.at[slot - 1, half, quarter],
+            act_recv.at[slot - 1, half, quarter],
+            z_pair if slot == 2 else y_pair,
+        )
+
+    def norm_half(half, state):
+        lanes = pl.ds(pl.multiple_of(half * HALF, HALF), HALF)
+        reads_at = pl.ds(pl.multiple_of(256 + half * 128, 128), 128)
+        for quarter in range(2):
+
+            @pl.loop(0, 2)
+            def _(i):
+                rows = pl.ds(pl.multiple_of(quarter * 128 + i * 64, 64), 64)
+                read = jnp.dot(sconv[rows, reads_at], state, preferred_element_type=jnp.float32)
+                gate = gate_ref[rows, lanes].astype(jnp.float32)
+                scan = part_ref[rows, lanes] + infl_ref[rows, lanes] * read
+                gated = scan * (gate * jax.nn.sigmoid(gate))
+                mean = jnp.sum(gated * gated, axis=1, keepdims=True) * (1.0 / HALF)
+                normed = gated * lax.rsqrt(mean + 1e-05) * gain_ref[:, lanes]
+                acts[0, half, rows, :] = normed.astype(jnp.bfloat16)
+
+            act_copy(2, half, quarter).start()
+            act_copy(1, half, quarter).start()
+
+    norm_half(y, state_own[...])
+    for q in range(4):
+        state_copies[q].wait_recv()
+    norm_half(1 - y, jnp.concatenate([state_in[q] for q in range(4)], axis=1))
+
+    def sum_copy(k, side, o):
+        to = h ^ o
+        rows = pl.ds(pl.multiple_of(to * 64, 64), 64)
+        return remote(
+            partial.at[k, side, rows],
+            sums_in.at[k, side, o - 1],
+            sum_send.at[k, side, o - 1],
+            sum_recv.at[k, side, o - 1],
+            s,
+            to,
+        )
+
+    def project(k, side):
+        weight = (weight_ref, weight_in)[side]
+
+        @pl.loop(0, 2)
+        def _(i):
+            lanes = pl.ds(pl.multiple_of(i * 256, 256), 256)
+            total = jnp.dot(
+                acts[k, 0], weight[0:HALF, lanes], preferred_element_type=jnp.float32
+            ) + jnp.dot(
+                acts[k, 1], weight[HALF:CHANNELS, lanes], preferred_element_type=jnp.float32
+            )
+            partial_own[k, side, :, lanes] = total
+            partial[k, side, :, lanes] = total.astype(jnp.bfloat16)
+
+        for o in (2, 3, 1):
+            sum_copy(k, side, o).start()
+
+    def final_part(k, side):
+        zt = z if k < 2 else z_far
+        yt = y if k % 2 == 0 else 1 - y
+        head = (z, z_near)[side]
+        target = 2 * zt + yt
+        stays = (target == s) & (head == h)
+        rows = pl.ds(pl.multiple_of(h * 64, 64), 64)
+        spot = pl.ds(pl.multiple_of(y * 512, 512), 512)
+        copy = remote(
+            final_out.at[k, side],
+            final_in.at[rows, spot],
+            final_send.at[k, side],
+            final_recv.at[y * 4 + h],
+            target,
+            head,
+        )
+        return rows, spot, stays, copy
+
+    def finish(k, side):
+        for o in (1, 2, 3):
+            sum_copy(k, side, o).wait_recv()
+        rows, spot, stays, copy = final_part(k, side)
+        total = partial_own[k, side, rows, :]
+        for o in range(3):
+            total = total + sums_in[k, side, o].astype(jnp.float32)
+        total = total.astype(jnp.bfloat16)
+        final_out[k, side] = total
+
+        @pl.when(stays)
+        def _():
+            final_in[rows, spot] = total
+
+        @pl.when(jnp.logical_not(stays))
+        def _():
+            copy.start()
+
+    def arrived(slot, half):
+        for quarter in range(2):
+            act_copy(slot, half, quarter).wait_recv()
+            if slot == 2:
+                act_copy(3, half, quarter).start()
+
+    weight_copy.wait()
+    project(0, 0)
+    arrived(1, 1 - y)
+    arrived(1, y)
+    project(1, 0)
+    finish(0, 0)
+    arrived(2, y)
+    for copy in weight_copies:
+        copy.wait_recv()
+    project(0, 1)
+    finish(1, 0)
+    project(1, 1)
+    finish(0, 1)
+    arrived(2, 1 - y)
+    project(2, 0)
+    finish(1, 1)
+    project(2, 1)
+    finish(2, 0)
+    arrived(3, 1 - y)
+    arrived(3, y)
+    project(3, 0)
+    finish(2, 1)
+    project(3, 1)
+    finish(3, 0)
+    finish(3, 1)
+
+    z_from = 2 * (h // 2) + z % 2
+    for y_from in range(2):
+        for h_from in range(4):
+            rows = slice(h_from * 64, h_from * 64 + 64)
+            spot = slice(y_from * 512, y_from * 512 + 512)
+            mine = (z_from == z) & (y_from == y) & (h_from == h)
+
+            @pl.when(jnp.logical_not(mine))
+            def _():
+                remote(
+                    final_out.at[0, 0],
+                    final_in.at[rows, spot],
+                    final_send.at[0, 0],
+                    final_recv.at[y_from * 4 + h_from],
+                    2 * z_from + y_from,
+                    h_from,
+                ).wait_recv()
+
+    out_ref[...] = final_in[...]
+
+    @pl.when(s < 7)
+    def _():
+        for copy in halo_copies:
+            copy.wait_send()
+
+    send_dep.wait_send()
+    send_fade.wait_send()
+    for q in range(4):
+        weight_copies[q].wait_send()
+        state_copies[q].wait_send()
+
+        @pl.when(z < 3)
+        def _():
+            chain_copies[q].wait_send()
+
+    for slot in (1, 2, 3):
+        for half in range(2):
+            for quarter in range(2):
+                act_copy(slot, half, quarter).wait_send()
+    for k in range(4):
+        for side in range(2):
+            for o in (1, 2, 3):
+                sum_copy(k, side, o).wait_send()
+            stays, copy = final_part(k, side)[2:]
+
+            @pl.when(jnp.logical_not(stays))
+            def _():
+                copy.wait_send()
+
+
+def on_device_fast(
+    inner_input,
+    state_input,
+    gate_input,
+    step_input,
+    decay_exponent,
+    skip_gain,
+    documents,
+    filter_inner,
+    filter_state,
+    norm_gain,
+    output_weight,
+):
+    vmem = pl.BlockSpec(memory_space=pltpu.VMEM)
+    smem = pl.BlockSpec(memory_space=pltpu.SMEM)
+    anywhere = pl.BlockSpec(memory_space=pl.ANY)
+    bf16, f32 = jnp.bfloat16, jnp.float32
+    dma = pltpu.SemaphoreType.DMA
+    return pl.pallas_call(
+        fused_kernel,
+        out_shape=jax.ShapeDtypeStruct((SPAN, 1024), bf16),
+        in_specs=[vmem] * 8 + [smem] + [anywhere] * 2,
+        out_specs=vmem,
+        scratch_shapes=[
+            pltpu.VMEM((SPAN, CHANNELS), bf16),
+            pltpu.VMEM((CHANNELS, 512), bf16),
+            pltpu.VMEM((CHANNELS, 512), bf16),
+            pltpu.VMEM((16, CHANNELS), bf16),
+            pltpu.VMEM((16, 512), bf16),
+            pltpu.VMEM((1, SPAN), jnp.int32),
+            pltpu.VMEM((SPAN + 16, 256), f32),
+            pltpu.VMEM((SPAN, CHANNELS), bf16),
+            pltpu.VMEM((SPAN, 512), bf16),
+            pltpu.VMEM((32, SPAN), f32),
+            pltpu.VMEM((32, SPAN), f32),
+            pltpu.VMEM((32, SPAN), f32),
+            pltpu.VMEM((32, SPAN), f32),
+            pltpu.VMEM((SPAN, HALF), bf16),
+            pltpu.VMEM((SPAN, CHANNELS), f32),
+            pltpu.VMEM((SPAN, CHANNELS), f32),
+            pltpu.VMEM((STATE, HALF), f32),
+            pltpu.VMEM((STATE, HALF), bf16),
+            pltpu.VMEM((STATE, HALF), bf16),
+            pltpu.VMEM((8, HALF), f32),
+            pltpu.VMEM((8, HALF), f32),
+            pltpu.VMEM((4, STATE, 256), bf16),
+            pltpu.VMEM((4, STATE, 256), bf16),
+            pltpu.VMEM((4, STATE, 256), bf16),
+            pltpu.VMEM((4, STATE, 256), bf16),
+            pltpu.VMEM((STATE, HALF), bf16),
+            pltpu.VMEM((4, 2, SPAN, HALF), bf16),
+            pltpu.VMEM((4, 2, SPAN, 512), bf16),
+            pltpu.VMEM((4, 2, SPAN, 512), f32),
+            pltpu.VMEM((4, 2, 3, 64, 512), bf16),
+            pltpu.VMEM((4, 2, 64, 512), bf16),
+            pltpu.VMEM((SPAN, 1024), bf16),
+            dma((2,)),
+            dma((2, 3)),
+            dma((2, 4)),
+            dma((4,)),
+            dma((2, 4)),
+            dma((2, 4)),
+            dma((3, 2, 2)),
+            dma((3, 2, 2)),
+            dma((4, 2, 3)),
+            dma((4, 2, 3)),
+            dma((4, 2)),
+            dma((8,)),
+        ],
+        compiler_params=pltpu.CompilerParams(
+            vmem_limit_bytes=56 * MIB, collective_id=0, has_side_effects=True
+        ),
+        name="layer",
+    )(
+        inner_input,
+        state_input.reshape(SPAN, 512),
+        step_input,
+        decay_exponent[None, :],
+        documents[None, :],
+        filter_inner,
+        filter_state.reshape(KERNEL, 512),
+        norm_gain[None, :],
+        skip_gain,
+        gate_input,
+        output_weight,
+    )
+
+
 def solution(mesh):
     placed = (
         P("seq", "head"),
@@ -170,6 +758,8 @@
         P("head"),
         P("head", "seq"),
     )
+    ways = dict(mesh.shape)
+    fast = ways["seq"] == 8 and ways["head"] == 4
     return jax.shard_map(
-        on_device, mesh=mesh, in_specs=placed, out_specs=P("seq", "head"), check_vma=False
-    )
+        on_device_fast if fast else on_device, mesh=mesh, in_specs=placed, out_specs=P("seq", "head"), check_vma=False
+    )

time: 457 us -> 134 us (0.29)
  waiting for transfers between devices: 349 us -> 0 us
  Pallas kernels: 0 us -> 129 us
  matrix products: 21.3 us -> 0 us
  other arithmetic: 20.6 us -> 0 us
  blocking collectives: 16.1 us -> 0 us
  local copies, waits for them, and re-layouts: 20.3 us -> 4.84 us
  between operations: 15.3 us -> 0.01 us
  starting transfers between devices: 10.4 us -> 0 us
    all_gather x2 -> x0, waiting for transfers between devices: 305 us -> none  [the longest x1 206 us: on_device(): lax.all_gather(output_weight, 'seq', axis=1, tiled=True)]
    pallas_call x0 -> x1, Pallas kernels: none -> 129 us  [on_device_fast(): pl.pallas_call(fused_kernel, out_shape=jax.ShapeDtypeStruct((SPAN, 1024),...]
    reduce_scatter x1 -> x0, waiting for transfers between devices: 43.8 us -> none  [on_device(): lax.psum_scatter(partial_value, 'head', scatter_dimension=1, tiled=True)]
    dot_general x5 -> x0, matrix products: 21.3 us -> none  [the longest x1 13.1 us: on_device(): jnp.dot(normed, lax.all_gather(output_weight, 'seq', axis=1, tiled=True),...]
    unnamed x1 -> x0, blocking collectives: 16.1 us -> none
    ppermute x3 -> x0, starting transfers between devices: 10.3 us -> none  [passed_along(): lax.ppermute(value, axis, [(source, source + steps) for source in range(i...]
    convert_element_type x5 -> x0, other arithmetic: 7.29 us -> none  [the longest x2 2.88 us: causal_conv(): return jax.nn.silu(running).astype(jnp.bfloat16)]
    mul x5 -> x0, local copies, waits for them, and re-layouts: 5.39 us -> none  [the longest x1 4.03 us: gated_norm(): mean_square = jnp.mean(grouped * grouped, axis=-1, keepdims=True)]
  transfers between devices with their start and end apart: 6 -> 0, of which waited for: 3 -> 0; matrix products, arithmetic and copies ran while one was open for 9% -> 0% of each run, Pallas kernels for 0% -> 0%
where the time goes in v2:
time: 134 us
  Pallas kernels  129 us (96%)
  local copies, waits for them, and re-layouts  4.84 us (4%)
    pallas_call x1, Pallas kernels, on_device_fast(): pl.pallas_call(fused_kernel, out_shape=jax.ShapeDtypeStruct((SPAN, 1024),...  129 us
    unnamed x3, local copies, waits for them, and re-layouts  4.84 us

profile of v2, /device:TPU:10, one launch (start us, length us, event | category | flops | bytes accessed | tf_op | source)
XLA Modules:
  0.0 133.7 jit_solution(6995504190695397279)
XLA Ops:
  0.0 1.3 copy.13
  1.3 1.7 %copy.12 = bf16[32,8,2,256]{3,1,2,0:T(8,128)(2,1)} copy(bf16[32,8,2,256]{3,2,1,0:T(2,128)(2,1)} %bitcast.8) | data formatting | bytes 524288
  3.0 128.8 %layer.1 = bf16[256,1024]{1,0:T(8,128)(2,1)} custom-call(bf16[256,2048]{1,0:T(8,128)(2,1)} %inner_ref.1, bf16[256,512]{1,0:T(8,128)(2,1)} %bitcast.7, f32[32,256]{1,0:T(8,128)} %step_ref.1, f32[1,32]{1,0:T(1,128)} %bitcast.13, s32[1,256]{1,0:T(1,128)} %bitcast.12, f32[4,2048]{1,0:T(4,128)} %filter_inner_ref.1, f32[4,512]{1,0:T(4,128)} %bitcast.9, ...), custom_call_target="tpu_custom_call" | custom-call | tf_op jit(solution)/shard_map/layer/pallas_call | solution.py:677
  131.8 1.9 %copy.15 = bf16[256,1024]{1,0:T(8,128)(2,1)} copy(bf16[256,1024]{1,0:T(8,128)(2,1)} %layer.1) | data formatting | bytes 1048576

commit v3 on v2

--- a/solution.py
+++ b/solution.py
@@ -210,6 +210,7 @@
     sums_in,
     final_out,
     final_in,
+    relay_in,
     local_sems,
     halo_sems,
     weight_sems,
@@ -222,6 +223,8 @@
     sum_recv,
     final_send,
     final_recv,
+    relay_send,
+    relay_recv,
 ):
     s = lax.axis_index("seq")
     h = lax.axis_index("head")
@@ -276,8 +279,8 @@
             copy.start()
 
     weight_copies = []
-    for i in range(4):
-        rows = pl.ds(i * 512, 512)
+    for i in range(8):
+        rows = pl.ds(i * 256, 256)
         weight_copies.append(
             remote(
                 weight_hbm.at[rows],
@@ -289,9 +292,13 @@
         )
     weight_copies[0].start()
 
+    @pl.when(z > 0)
+    def _():
+        weight_copies[1].start()
+
     @pl.when(z % 2 == 1)
     def _():
-        for copy in weight_copies[1:]:
+        for copy in weight_copies[2:]:
             copy.start()
 
     @pl.when(s == 0)
@@ -374,36 +381,19 @@
             convolve(inner_ref, halo_inner, at, filter_inner_ref, conv)
 
         writes = sconv[:, pl.ds(pl.multiple_of(group * 128, 128), 128)]
-        reads = sconv[:, pl.ds(pl.multiple_of(256 + group * 128, 128), 128)]
-        scores = lax.dot_general(
-            reads, writes, (((1,), (1,)), ((), ())), preferred_element_type=jnp.float32
-        )
-        scores = jnp.where(linked, scores, 0.0)
         heads = pl.ds(pl.multiple_of(group * 16, 16), 16)
-        cums = cum_rows[heads, :]
-        steps = step_rows[heads, :]
-        cum_cols = cums.T
         in_cols = in_rows[heads, :].T
         close_cols = close_rows[heads, :].T
         for pair in range(8):
             first = pair * 2
             at = pl.ds(pl.multiple_of(base + pair * 128, 128), 128)
-            x = conv[:, at]
-
-            def mixed(j):
-                spread = jnp.minimum(cum_cols[:, j : j + 1] - cums[j : j + 1, :], 0.0)
-                mixing = (jnp.exp(spread) * scores * steps[j : j + 1, :]).astype(jnp.bfloat16)
-                return jnp.dot(mixing, x, preferred_element_type=jnp.float32)
 
             def both(cols):
                 return jnp.where(low, cols[:, first : first + 1], cols[:, first + 1 : first + 2])
 
-            x32 = x.astype(jnp.float32)
-            gain = jnp.where(low, skip_ref[group * 16 + first], skip_ref[group * 16 + first + 1])
-            part_ref[:, at] = jnp.where(low, mixed(first), mixed(first + 1)) + gain * x32
-            weighted[:, pair * 128 : pair * 128 + 128] = (x32 * both(close_cols)).astype(
-                jnp.bfloat16
-            )
+            weighted[:, pair * 128 : pair * 128 + 128] = (
+                conv[:, at].astype(jnp.float32) * both(close_cols)
+            ).astype(jnp.bfloat16)
             infl_ref[:, at] = both(in_cols)
         dep_ref[...] = lax.dot_general(
             writes, weighted[...], (((0,), (0,)), ((), ())), preferred_element_type=jnp.float32
@@ -416,12 +406,37 @@
             send_fade.start()
             send_dep.start()
 
+    def mixing_of(group):
+        base = group * HALF
+        writes = sconv[:, pl.ds(pl.multiple_of(group * 128, 128), 128)]
+        reads = sconv[:, pl.ds(pl.multiple_of(256 + group * 128, 128), 128)]
+        scores = lax.dot_general(
+            reads, writes, (((1,), (1,)), ((), ())), preferred_element_type=jnp.float32
+        )
+        scores = jnp.where(linked, scores, 0.0)
+        heads = pl.ds(pl.multiple_of(group * 16, 16), 16)
+        cums = cum_rows[heads, :]
+        steps = step_rows[heads, :]
+        cum_cols = cums.T
+        for pair in range(8):
+            first = pair * 2
+            at = pl.ds(pl.multiple_of(base + pair * 128, 128), 128)
+            x = conv[:, at]
+
+            def mixed(j):
+                spread = jnp.minimum(cum_cols[:, j : j + 1] - cums[j : j + 1, :], 0.0)
+                mixing = (jnp.exp(spread) * scores * steps[j : j + 1, :]).astype(jnp.bfloat16)
+                return jnp.dot(mixing, x, preferred_element_type=jnp.float32)
+
+            gain = jnp.where(low, skip_ref[group * 16 + first], skip_ref[group * 16 + first + 1])
+            part_ref[:, at] = jnp.where(low, mixed(first), mixed(first + 1)) + gain * x.astype(
+                jnp.float32
+            )
+
     @pl.when(z == 0)
     def _():
         chain_in[...] = jnp.zeros_like(chain_in)
 
-    send_fade.wait_recv()
-    send_dep.wait_recv()
     is_first = y == 0
     chain_copies = [
         remote(
@@ -437,39 +452,58 @@
         remote(state_out.at[q], state_in.at[q], state_sems.at[0, q], state_sems.at[1, q], y_pair)
         for q in range(4)
     ]
-    for q in range(4):
-        lanes = pl.ds(pl.multiple_of(y * HALF + q * 256, 256), 256)
-        here = slice(q * 256, q * 256 + 256)
-        dep_own = dep_ref[:, here]
-        dep_other = dep_in[:, here].astype(jnp.float32)
-        fade_own = infl_ref[SPAN - 8 : SPAN, lanes][7:8]
-        fade_other = fade_in[7:8, here]
-        dep_0 = jnp.where(is_first, dep_own, dep_other)
-        dep_1 = jnp.where(is_first, dep_other, dep_own)
-        fade_0 = jnp.where(is_first, fade_own, fade_other)
-        fade_1 = jnp.where(is_first, fade_other, fade_own)
-        slab = fade_1 * dep_0 + dep_1
-        slab_fade = fade_0 * fade_1
-
-        @pl.when(z > 0)
+    def chain():
+        send_fade.wait_recv()
+        send_dep.wait_recv()
+        for q in range(4):
+            lanes = pl.ds(pl.multiple_of(y * HALF + q * 256, 256), 256)
+            here = slice(q * 256, q * 256 + 256)
+            dep_own = dep_ref[:, here]
+            dep_other = dep_in[:, here].astype(jnp.float32)
+            fade_own = infl_ref[SPAN - 8 : SPAN, lanes][7:8]
+            fade_other = fade_in[7:8, here]
+            dep_0 = jnp.where(is_first, dep_own, dep_other)
+            dep_1 = jnp.where(is_first, dep_other, dep_own)
+            fade_0 = jnp.where(is_first, fade_own, fade_other)
+            fade_1 = jnp.where(is_first, fade_other, fade_own)
+            slab = fade_1 * dep_0 + dep_1
+            slab_fade = fade_0 * fade_1
+
+            @pl.when(z > 0)
+            def _():
+                chain_copies[q].wait_recv()
+
+            entering_0 = chain_in[q].astype(jnp.float32)
+            chain_out[q] = (slab_fade * entering_0 + slab).astype(jnp.bfloat16)
+
+            @pl.when(z < 3)
+            def _():
+                chain_copies[q].start()
+
+            entering_1 = fade_0 * entering_0 + dep_0
+            state_own[:, here] = jnp.where(is_first, entering_0, entering_1).astype(jnp.bfloat16)
+            state_out[q] = jnp.where(is_first, entering_1, entering_0).astype(jnp.bfloat16)
+            state_copies[q].start()
+
+    @pl.loop(0, 3)
+    def _(phase):
+        late = jnp.where(z >= 2, 1, 0)
+
+        @pl.when(phase != 1 + late)
         def _():
-            chain_copies[q].wait_recv()
-
-        entering_0 = chain_in[q].astype(jnp.float32)
-        chain_out[q] = (slab_fade * entering_0 + slab).astype(jnp.bfloat16)
-
-        @pl.when(z < 3)
+            mixing_of(jnp.where(phase == 0, 1 - y, y))
+
+        @pl.when(phase == 1 + late)
         def _():
-            chain_copies[q].start()
-
-        entering_1 = fade_0 * entering_0 + dep_0
-        state_own[:, here] = jnp.where(is_first, entering_0, entering_1).astype(jnp.bfloat16)
-        state_out[q] = jnp.where(is_first, entering_1, entering_0).astype(jnp.bfloat16)
-        state_copies[q].start()
+            chain()
+
+    @pl.when(z == 0)
+    def _():
+        weight_copies[1].start()
 
     @pl.when(z % 2 == 0)
     def _():
-        for copy in weight_copies[1:]:
+        for copy in weight_copies[2:]:
             copy.start()
 
     gate_copy.wait()
@@ -538,41 +572,63 @@
         for o in (2, 3, 1):
             sum_copy(k, side, o).start()
 
-    def final_part(k, side):
-        zt = z if k < 2 else z_far
-        yt = y if k % 2 == 0 else 1 - y
-        head = (z, z_near)[side]
-        target = 2 * zt + yt
-        stays = (target == s) & (head == h)
-        rows = pl.ds(pl.multiple_of(h * 64, 64), 64)
-        spot = pl.ds(pl.multiple_of(y * 512, 512), 512)
-        copy = remote(
-            final_out.at[k, side],
-            final_in.at[rows, spot],
+    rows_own = pl.ds(pl.multiple_of(h * 64, 64), 64)
+    spot_own = pl.ds(pl.multiple_of(y * 512, 512), 512)
+
+    def final_copy(source, k, side, target, head):
+        return remote(
+            source,
+            final_in.at[rows_own, spot_own],
             final_send.at[k, side],
             final_recv.at[y * 4 + h],
             target,
             head,
         )
-        return rows, spot, stays, copy
+
+    def hand_over(k, side, source):
+        z_of = z if k < 2 else z_far
+        head = z_of if side == 0 else z_of + 1 - 2 * (z_of % 2)
+        copy = final_copy(source, k, side, s if k % 2 == 0 else y_pair, head)
+        return copy, (head == h if k % 2 == 0 else None)
+
+    def deliver(k, side, source):
+        copy, stays = hand_over(k, side, source)
+        if stays is None:
+            copy.start()
+            return
+
+        @pl.when(stays)
+        def _():
+            final_in[rows_own, spot_own] = source[...]
+
+        @pl.when(jnp.logical_not(stays))
+        def _():
+            copy.start()
+
+    def relay_copy(k, side):
+        return remote(
+            final_out.at[k, side],
+            relay_in.at[k - 2, side],
+            relay_send.at[k - 2, side],
+            relay_recv.at[k - 2, side],
+            z_pair,
+        )
+
+    def pass_on(k, side):
+        relay_copy(k, side).wait_recv()
+        deliver(k, side, relay_in.at[k - 2, side])
 
     def finish(k, side):
         for o in (1, 2, 3):
             sum_copy(k, side, o).wait_recv()
-        rows, spot, stays, copy = final_part(k, side)
-        total = partial_own[k, side, rows, :]
+        total = partial_own[k, side, rows_own, :]
         for o in range(3):
             total = total + sums_in[k, side, o].astype(jnp.float32)
-        total = total.astype(jnp.bfloat16)
-        final_out[k, side] = total
-
-        @pl.when(stays)
-        def _():
-            final_in[rows, spot] = total
-
-        @pl.when(jnp.logical_not(stays))
-        def _():
-            copy.start()
+        final_out[k, side] = total.astype(jnp.bfloat16)
+        if k < 2:
+            deliver(k, side, final_out.at[k, side])
+        else:
+            relay_copy(k, side).start()
 
     def arrived(slot, half):
         for quarter in range(2):
@@ -605,13 +661,16 @@
     project(3, 1)
     finish(3, 0)
     finish(3, 1)
+    for k in (2, 3):
+        for side in range(2):
+            pass_on(k, side)
 
     z_from = 2 * (h // 2) + z % 2
     for y_from in range(2):
         for h_from in range(4):
             rows = slice(h_from * 64, h_from * 64 + 64)
             spot = slice(y_from * 512, y_from * 512 + 512)
-            mine = (z_from == z) & (y_from == y) & (h_from == h)
+            mine = (y_from == y) & (h_from == h)
 
             @pl.when(jnp.logical_not(mine))
             def _():
@@ -633,8 +692,9 @@
 
     send_dep.wait_send()
     send_fade.wait_send()
+    for copy in weight_copies:
+        copy.wait_send()
     for q in range(4):
-        weight_copies[q].wait_send()
         state_copies[q].wait_send()
 
         @pl.when(z < 3)
@@ -649,11 +709,17 @@
         for side in range(2):
             for o in (1, 2, 3):
                 sum_copy(k, side, o).wait_send()
-            stays, copy = final_part(k, side)[2:]
-
-            @pl.when(jnp.logical_not(stays))
-            def _():
+            if k >= 2:
+                relay_copy(k, side).wait_send()
+            source = final_out.at[k, side] if k < 2 else relay_in.at[k - 2, side]
+            copy, stays = hand_over(k, side, source)
+            if stays is None:
                 copy.wait_send()
+            else:
+
+                @pl.when(jnp.logical_not(stays))
+                def _():
+                    copy.wait_send()
 
 
 def on_device_fast(
@@ -712,9 +778,10 @@
             pltpu.VMEM((4, 2, 3, 64, 512), bf16),
             pltpu.VMEM((4, 2, 64, 512), bf16),
             pltpu.VMEM((SPAN, 1024), bf16),
+            pltpu.VMEM((2, 2, 64, 512), bf16),
             dma((2,)),
             dma((2, 3)),
-            dma((2, 4)),
+            dma((2, 8)),
             dma((4,)),
             dma((2, 4)),
             dma((2, 4)),
@@ -724,6 +791,8 @@
             dma((4, 2, 3)),
             dma((4, 2)),
             dma((8,)),
+            dma((2, 2)),
+            dma((2, 2)),
         ],
         compiler_params=pltpu.CompilerParams(
             vmem_limit_bytes=56 * MIB, collective_id=0, has_side_effects=True

time: 134 us -> 132 us (0.985)
  Pallas kernels: 129 us -> 127 us
    pallas_call x1, Pallas kernels: 129 us -> 127 us  [on_device_fast(): pl.pallas_call(fused_kernel, out_shape=jax.ShapeDtypeStruct((SPAN, 1024),...]
where the time goes in v3:
time: 132 us; the launch traced here: 131 us
  Pallas kernels  127 us (96%)
  local copies, waits for them, and re-layouts  4.84 us (4%)
    pallas_call x1, Pallas kernels, on_device_fast(): pl.pallas_call(fused_kernel, out_shape=jax.ShapeDtypeStruct((SPAN, 1024),...  127 us
    unnamed x3, local copies, waits for them, and re-layouts  4.84 us

profile of v3, /device:TPU:10, one launch (start us, length us, event | category | flops | bytes accessed | tf_op | source)
XLA Modules:
  0.0 131.4 jit_solution(7149481985148089863)
XLA Ops:
  0.0 1.3 copy.13
  1.3 1.7 %copy.12 = bf16[32,8,2,256]{3,1,2,0:T(8,128)(2,1)} copy(bf16[32,8,2,256]{3,2,1,0:T(2,128)(2,1)} %bitcast.8) | data formatting | bytes 524288
  3.0 126.6 %layer.1 = bf16[256,1024]{1,0:T(8,128)(2,1)} custom-call(bf16[256,2048]{1,0:T(8,128)(2,1)} %inner_ref.1, bf16[256,512]{1,0:T(8,128)(2,1)} %bitcast.7, f32[32,256]{1,0:T(8,128)} %step_ref.1, f32[1,32]{1,0:T(1,128)} %bitcast.13, s32[1,256]{1,0:T(1,128)} %bitcast.12, f32[4,2048]{1,0:T(4,128)} %filter_inner_ref.1, f32[4,512]{1,0:T(4,128)} %bitcast.9, ...), custom_call_target="tpu_custom_call" | custom-call | tf_op jit(solution)/shard_map/layer/pallas_call | solution.py:743
  129.6 1.9 %copy.15 = bf16[256,1024]{1,0:T(8,128)(2,1)} copy(bf16[256,1024]{1,0:T(8,128)(2,1)} %layer.1) | data formatting | bytes 1048576

commit v4 on v3

--- a/solution.py
+++ b/solution.py
@@ -210,7 +210,6 @@
     sums_in,
     final_out,
     final_in,
-    relay_in,
     local_sems,
     halo_sems,
     weight_sems,
@@ -223,8 +222,6 @@
     sum_recv,
     final_send,
     final_recv,
-    relay_send,
-    relay_recv,
 ):
     s = lax.axis_index("seq")
     h = lax.axis_index("head")
@@ -295,10 +292,11 @@
     @pl.when(z > 0)
     def _():
         weight_copies[1].start()
+        weight_copies[2].start()
 
     @pl.when(z % 2 == 1)
     def _():
-        for copy in weight_copies[2:]:
+        for copy in weight_copies[3:]:
             copy.start()
 
     @pl.when(s == 0)
@@ -500,10 +498,11 @@
     @pl.when(z == 0)
     def _():
         weight_copies[1].start()
+        weight_copies[2].start()
 
     @pl.when(z % 2 == 0)
     def _():
-        for copy in weight_copies[2:]:
+        for copy in weight_copies[3:]:
             copy.start()
 
     gate_copy.wait()
@@ -575,48 +574,18 @@
     rows_own = pl.ds(pl.multiple_of(h * 64, 64), 64)
     spot_own = pl.ds(pl.multiple_of(y * 512, 512), 512)
 
-    def final_copy(source, k, side, target, head):
-        return remote(
-            source,
+    def final_part(k, side):
+        zt = z if k < 2 else z_far
+        head = z if side == 0 else z_near
+        copy = remote(
+            final_out.at[k, side],
             final_in.at[rows_own, spot_own],
             final_send.at[k, side],
             final_recv.at[y * 4 + h],
-            target,
+            2 * zt + (y if k % 2 == 0 else 1 - y),
             head,
         )
-
-    def hand_over(k, side, source):
-        z_of = z if k < 2 else z_far
-        head = z_of if side == 0 else z_of + 1 - 2 * (z_of % 2)
-        copy = final_copy(source, k, side, s if k % 2 == 0 else y_pair, head)
-        return copy, (head == h if k % 2 == 0 else None)
-
-    def deliver(k, side, source):
-        copy, stays = hand_over(k, side, source)
-        if stays is None:
-            copy.start()
-            return
-
-        @pl.when(stays)
-        def _():
-            final_in[rows_own, spot_own] = source[...]
-
-        @pl.when(jnp.logical_not(stays))
-        def _():
-            copy.start()
-
-    def relay_copy(k, side):
-        return remote(
-            final_out.at[k, side],
-            relay_in.at[k - 2, side],
-            relay_send.at[k - 2, side],
-            relay_recv.at[k - 2, side],
-            z_pair,
-        )
-
-    def pass_on(k, side):
-        relay_copy(k, side).wait_recv()
-        deliver(k, side, relay_in.at[k - 2, side])
+        return copy, (head == h if k == 0 else None)
 
     def finish(k, side):
         for o in (1, 2, 3):
@@ -625,10 +594,18 @@
         for o in range(3):
             total = total + sums_in[k, side, o].astype(jnp.float32)
         final_out[k, side] = total.astype(jnp.bfloat16)
-        if k < 2:
-            deliver(k, side, final_out.at[k, side])
-        else:
-            relay_copy(k, side).start()
+        copy, stays = final_part(k, side)
+        if stays is None:
+            copy.start()
+            return
+
+        @pl.when(stays)
+        def _():
+            final_in[rows_own, spot_own] = final_out[k, side]
+
+        @pl.when(jnp.logical_not(stays))
+        def _():
+            copy.start()
 
     def arrived(slot, half):
         for quarter in range(2):
@@ -661,16 +638,13 @@
     project(3, 1)
     finish(3, 0)
     finish(3, 1)
-    for k in (2, 3):
-        for side in range(2):
-            pass_on(k, side)
 
     z_from = 2 * (h // 2) + z % 2
     for y_from in range(2):
         for h_from in range(4):
             rows = slice(h_from * 64, h_from * 64 + 64)
             spot = slice(y_from * 512, y_from * 512 + 512)
-            mine = (y_from == y) & (h_from == h)
+            mine = (z_from == z) & (y_from == y) & (h_from == h)
 
             @pl.when(jnp.logical_not(mine))
             def _():
@@ -709,10 +683,7 @@
         for side in range(2):
             for o in (1, 2, 3):
                 sum_copy(k, side, o).wait_send()
-            if k >= 2:
-                relay_copy(k, side).wait_send()
-            source = final_out.at[k, side] if k < 2 else relay_in.at[k - 2, side]
-            copy, stays = hand_over(k, side, source)
+            copy, stays = final_part(k, side)
             if stays is None:
                 copy.wait_send()
             else:
@@ -778,7 +749,6 @@
             pltpu.VMEM((4, 2, 3, 64, 512), bf16),
             pltpu.VMEM((4, 2, 64, 512), bf16),
             pltpu.VMEM((SPAN, 1024), bf16),
-            pltpu.VMEM((2, 2, 64, 512), bf16),
             dma((2,)),
             dma((2, 3)),
             dma((2, 8)),
@@ -791,8 +761,6 @@
             dma((4, 2, 3)),
             dma((4, 2)),
             dma((8,)),
-            dma((2, 2)),
-            dma((2, 2)),
         ],
         compiler_params=pltpu.CompilerParams(
             vmem_limit_bytes=56 * MIB, collective_id=0, has_side_effects=True

time: 132 us -> 129 us (0.977)
  Pallas kernels: 127 us -> 124 us
    pallas_call x1, Pallas kernels: 127 us -> 124 us  [on_device_fast(): pl.pallas_call(fused_kernel, out_shape=jax.ShapeDtypeStruct((SPAN, 1024),...]
where the time goes in v4:
time: 129 us
  Pallas kernels  124 us (96%)
  local copies, waits for them, and re-layouts  4.84 us (4%)
    pallas_call x1, Pallas kernels, on_device_fast(): pl.pallas_call(fused_kernel, out_shape=jax.ShapeDtypeStruct((SPAN, 1024),...  124 us
    unnamed x3, local copies, waits for them, and re-layouts  4.84 us

profile of v4, /device:TPU:10, one launch (start us, length us, event | category | flops | bytes accessed | tf_op | source)
XLA Modules:
  0.0 128.8 jit_solution(16928010260198264722)
XLA Ops:
  0.0 1.3 %copy.13 = f32[1,4,2,256]{3,1,2,0:T(4,128)} copy(f32[1,4,2,256]{3,2,1,0:T(2,128)} %bitcast.11) | data formatting | bytes 16384
  1.3 1.7 %copy.12 = bf16[32,8,2,256]{3,1,2,0:T(8,128)(2,1)} copy(bf16[32,8,2,256]{3,2,1,0:T(2,128)(2,1)} %bitcast.8) | data formatting | bytes 524288
  3.0 124.0 %layer.1 = bf16[256,1024]{1,0:T(8,128)(2,1)} custom-call(bf16[256,2048]{1,0:T(8,128)(2,1)} %inner_ref.1, bf16[256,512]{1,0:T(8,128)(2,1)} %bitcast.7, f32[32,256]{1,0:T(8,128)} %step_ref.1, f32[1,32]{1,0:T(1,128)} %bitcast.13, s32[1,256]{1,0:T(1,128)} %bitcast.12, f32[4,2048]{1,0:T(4,128)} %filter_inner_ref.1, f32[4,512]{1,0:T(4,128)} %bitcast.9, ...), custom_call_target="tpu_custom_call" | custom-call | tf_op jit(solution)/shard_map/layer/pallas_call | solution.py:714
  127.0 1.9 %copy.15 = bf16[256,1024]{1,0:T(8,128)(2,1)} copy(bf16[256,1024]{1,0:T(8,128)(2,1)} %layer.1) | data formatting | bytes 1048576

commit v5 on v4

--- a/solution.py
+++ b/solution.py
@@ -351,15 +351,20 @@
         lanes = pl.ds(at, 256)
         ext[0:16, :] = halo[:, lanes].astype(jnp.float32)
         ext[16:272, :] = source[:, lanes].astype(jnp.float32)
-        running = marks[:, 3:4] * (ext[13:269, :] * taps[0:1, lanes])
-        running = running + marks[:, 2:3] * (ext[14:270, :] * taps[1:2, lanes])
-        running = running + marks[:, 1:2] * (ext[15:271, :] * taps[2:3, lanes])
-        running = running + ext[16:272, :] * taps[3:4, lanes]
+        running = marks[:, 3:4] * (ext[13:269, :] * taps(0, lanes))
+        running = running + marks[:, 2:3] * (ext[14:270, :] * taps(1, lanes))
+        running = running + marks[:, 1:2] * (ext[15:271, :] * taps(2, lanes))
+        running = running + ext[16:272, :] * taps(3, lanes)
         target[:, lanes] = (running * jax.nn.sigmoid(running)).astype(jnp.bfloat16)
 
-    @pl.loop(0, 2)
-    def _(i):
-        convolve(state_ref, halo_state, pl.multiple_of(i * 256, 256), filter_state_ref, sconv)
+    for i in range(2):
+        convolve(
+            state_ref,
+            halo_state,
+            i * 256,
+            lambda k, lanes, i=i: filter_state_ref[k, i : i + 1, :],
+            sconv,
+        )
 
     linked = (marks[:, 0:1] == documents) & (row_at >= col_at)
     low = lax.broadcasted_iota(jnp.int32, (SPAN, 128), 1) < HEAD_DIM
@@ -376,7 +381,13 @@
         @pl.loop(0, 4)
         def _(i):
             at = pl.multiple_of(base + i * 256, 256)
-            convolve(inner_ref, halo_inner, at, filter_inner_ref, conv)
+            convolve(
+                inner_ref,
+                halo_inner,
+                at,
+                lambda k, lanes: filter_inner_ref[k : k + 1, lanes],
+                conv,
+            )
 
         writes = sconv[:, pl.ds(pl.multiple_of(group * 128, 128), 128)]
         heads = pl.ds(pl.multiple_of(group * 16, 16), 16)
@@ -620,17 +631,34 @@
     project(1, 0)
     finish(0, 0)
     arrived(2, y)
-    for copy in weight_copies:
-        copy.wait_recv()
-    project(0, 1)
     finish(1, 0)
-    project(1, 1)
-    finish(0, 1)
+
+    def first_blocks():
+        for copy in weight_copies:
+            copy.wait_recv()
+        project(0, 1)
+        project(1, 1)
+        finish(0, 1)
+
+    @pl.when(z < 3)
+    def _():
+        first_blocks()
+
     arrived(2, 1 - y)
     project(2, 0)
-    finish(1, 1)
+
+    @pl.when(z < 3)
+    def _():
+        finish(1, 1)
+
+    finish(2, 0)
+
+    @pl.when(z == 3)
+    def _():
+        first_blocks()
+        finish(1, 1)
+
     project(2, 1)
-    finish(2, 0)
     arrived(3, 1 - y)
     arrived(3, y)
     project(3, 0)
@@ -773,7 +801,7 @@
         decay_exponent[None, :],
         documents[None, :],
         filter_inner,
-        filter_state.reshape(KERNEL, 512),
+        filter_state,
         norm_gain[None, :],
         skip_gain,
         gate_input,

time: 129 us -> 127 us (0.984)
  local copies, waits for them, and re-layouts: 4.84 us -> 3.55 us
    unnamed x3 -> x2, local copies, waits for them, and re-layouts: 4.84 us -> 3.55 us
where the time goes in v5:
time: 127 us; the launch traced here: 126 us
  Pallas kernels  123 us (97%)
  local copies, waits for them, and re-layouts  3.55 us (3%)
    pallas_call x1, Pallas kernels, on_device_fast(): pl.pallas_call(fused_kernel, out_shape=jax.ShapeDtypeStruct((SPAN, 1024),...  123 us
    unnamed x2, local copies, waits for them, and re-layouts  3.55 us

profile of v5, /device:TPU:10, one launch (start us, length us, event | category | flops | bytes accessed | tf_op | source)
XLA Modules:
  0.0 126.4 jit_solution(10022506064808012485)
XLA Ops:
  0.0 1.7 %copy.12 = bf16[32,8,2,256]{3,1,2,0:T(8,128)(2,1)} copy(bf16[32,8,2,256]{3,2,1,0:T(2,128)(2,1)} %bitcast.6) | data formatting | bytes 524288
  1.7 122.8 %layer.1 = bf16[256,1024]{1,0:T(8,128)(2,1)} custom-call(bf16[256,2048]{1,0:T(8,128)(2,1)} %inner_ref.1, bf16[256,512]{1,0:T(8,128)(2,1)} %bitcast.5, f32[32,256]{1,0:T(8,128)} %step_ref.1, f32[1,32]{1,0:T(1,128)} %bitcast.9, s32[1,256]{1,0:T(1,128)} %bitcast.8, f32[4,2048]{1,0:T(4,128)} %filter_inner_ref.1, f32[4,2,256]{2,1,0:T(2,128)} %filter_state_ref.1, ...), custom_call_target="tpu_custom_call" | custom-call | tf_op jit(solution)/shard_map/layer/pallas_call | solution.py:742
  124.5 1.9 %copy.14 = bf16[256,1024]{1,0:T(8,128)(2,1)} copy(bf16[256,1024]{1,0:T(8,128)(2,1)} %layer.1) | data formatting | bytes 1048576

commit v6 on v5

--- a/solution.py
+++ b/solution.py
@@ -222,6 +222,16 @@
     sum_recv,
     final_send,
     final_recv,
+    weight_extra,
+    extra_part,
+    extra_own,
+    extra_sums,
+    extra_out,
+    extra_weight_sems,
+    extra_send,
+    extra_recv,
+    extra_final_send,
+    extra_final_recv,
 ):
     s = lax.axis_index("seq")
     h = lax.axis_index("head")
@@ -275,29 +285,48 @@
         for copy in halo_copies:
             copy.start()
 
-    weight_copies = []
-    for i in range(8):
-        rows = pl.ds(i * 256, 256)
-        weight_copies.append(
-            remote(
-                weight_hbm.at[rows],
-                weight_in.at[rows],
-                weight_sems.at[0, i],
-                weight_sems.at[1, i],
-                2 * z_near + y,
+    def weight_parts(wide):
+        parts = []
+        for i in range(8):
+            at = (pl.ds(i * 256, 256), pl.ds(0, wide))
+            parts.append(
+                remote(
+                    weight_hbm.at[at],
+                    weight_in.at[at],
+                    weight_sems.at[0, i],
+                    weight_sems.at[1, i],
+                    2 * z_near + y,
+                )
             )
-        )
-    weight_copies[0].start()
-
-    @pl.when(z > 0)
-    def _():
-        weight_copies[1].start()
-        weight_copies[2].start()
+        return parts
+
+    weight_whole, weight_less = weight_parts(512), weight_parts(384)
+    weight_aside = remote(
+        weight_hbm.at[:, pl.ds(384, 128)],
+        weight_extra,
+        extra_weight_sems.at[0],
+        extra_weight_sems.at[1],
+        2 + y,
+    )
+
+    @pl.when(z == 2)
+    def _():
+        for copy in weight_less[:3]:
+            copy.start()
+        weight_aside.start()
+
+    @pl.when(z == 0)
+    def _():
+        weight_whole[0].start()
 
     @pl.when(z % 2 == 1)
     def _():
-        for copy in weight_copies[3:]:
+        for copy in weight_whole:
             copy.start()
+
+    @pl.when(z == 3)
+    def _():
+        weight_in[:, 384:512] = jnp.zeros((CHANNELS, 128), jnp.bfloat16)
 
     @pl.when(s == 0)
     def _():
@@ -508,12 +537,12 @@
 
     @pl.when(z == 0)
     def _():
-        weight_copies[1].start()
-        weight_copies[2].start()
-
-    @pl.when(z % 2 == 0)
-    def _():
-        for copy in weight_copies[3:]:
+        for copy in weight_whole[1:]:
+            copy.start()
+
+    @pl.when(z == 2)
+    def _():
+        for copy in weight_less[3:]:
             copy.start()
 
     gate_copy.wait()
@@ -585,18 +614,26 @@
     rows_own = pl.ds(pl.multiple_of(h * 64, 64), 64)
     spot_own = pl.ds(pl.multiple_of(y * 512, 512), 512)
 
-    def final_part(k, side):
-        zt = z if k < 2 else z_far
-        head = z if side == 0 else z_near
-        copy = remote(
-            final_out.at[k, side],
-            final_in.at[rows_own, spot_own],
+    def final_target(k):
+        return 2 * (z if k < 2 else z_far) + (y if k % 2 == 0 else 1 - y)
+
+    def final_part(k, side, wide):
+        spot = pl.ds(pl.multiple_of(y * 512, 512), wide)
+        return remote(
+            final_out.at[k, side, :, pl.ds(0, wide)],
+            final_in.at[rows_own, spot],
             final_send.at[k, side],
             final_recv.at[y * 4 + h],
-            2 * zt + (y if k % 2 == 0 else 1 - y),
-            head,
-        )
-        return copy, (head == h if k == 0 else None)
+            final_target(k),
+            z if side == 0 else z_near,
+        )
+
+    def final_cases(k, side):
+        head = z if side == 0 else z_near
+        leaves = head != h if k == 0 else head >= 0
+        if side == 0:
+            return [(leaves, 512)]
+        return [(leaves & (z < 3), 512), (leaves & (z == 3), 384)]
 
     def finish(k, side):
         for o in (1, 2, 3):
@@ -605,18 +642,77 @@
         for o in range(3):
             total = total + sums_in[k, side, o].astype(jnp.float32)
         final_out[k, side] = total.astype(jnp.bfloat16)
-        copy, stays = final_part(k, side)
-        if stays is None:
-            copy.start()
+        for case, wide in final_cases(k, side):
+
+            @pl.when(case)
+            def _():
+                final_part(k, side, wide).start()
+
+        if k == 0:
+            stays = (z if side == 0 else z_near) == h
+            less = (z == 3) & (side == 1)
+
+            @pl.when(stays & jnp.logical_not(less))
+            def _():
+                final_in[rows_own, spot_own] = final_out[k, side]
+
+            @pl.when(stays & less)
+            def _():
+                spot = pl.ds(pl.multiple_of(y * 512, 512), 384)
+                final_in[rows_own, spot] = final_out[k, side, :, 0:384]
+
+    spot_extra = pl.ds(pl.multiple_of(y * 512 + 384, 128), 128)
+
+    def extra_copy(k, o):
+        to = h ^ o
+        return remote(
+            extra_part.at[k, pl.ds(pl.multiple_of(to * 64, 64), 64)],
+            extra_sums.at[k, o - 1],
+            extra_send.at[k, o - 1],
+            extra_recv.at[k, o - 1],
+            s,
+            to,
+        )
+
+    def project_extra(k):
+        total = jnp.dot(
+            acts[k, 0], weight_extra[0:HALF, :], preferred_element_type=jnp.float32
+        ) + jnp.dot(
+            acts[k, 1], weight_extra[HALF:CHANNELS, :], preferred_element_type=jnp.float32
+        )
+        extra_own[k] = total
+        extra_part[k] = total.astype(jnp.bfloat16)
+        for o in (2, 3, 1):
+            extra_copy(k, o).start()
+
+    def extra_final(k):
+        return remote(
+            extra_out.at[k],
+            final_in.at[rows_own, spot_extra],
+            extra_final_send.at[k],
+            extra_final_recv.at[y * 4 + h],
+            final_target(k),
+            2,
+        )
+
+    def finish_extra(k):
+        for o in (1, 2, 3):
+            extra_copy(k, o).wait_recv()
+        total = extra_own[k, rows_own, :]
+        for o in range(3):
+            total = total + extra_sums[k, o].astype(jnp.float32)
+        extra_out[k] = total.astype(jnp.bfloat16)
+        if k > 0:
+            extra_final(k).start()
             return
 
-        @pl.when(stays)
+        @pl.when(h != 2)
         def _():
-            final_in[rows_own, spot_own] = final_out[k, side]
-
-        @pl.when(jnp.logical_not(stays))
+            extra_final(k).start()
+
+        @pl.when(h == 2)
         def _():
-            copy.start()
+            final_in[rows_own, spot_extra] = extra_out[k]
 
     def arrived(slot, half):
         for quarter in range(2):
@@ -633,8 +729,8 @@
     arrived(2, y)
     finish(1, 0)
 
-    def first_blocks():
-        for copy in weight_copies:
+    def first_blocks(copies):
+        for copy in copies:
             copy.wait_recv()
         project(0, 1)
         project(1, 1)
@@ -642,7 +738,13 @@
 
     @pl.when(z < 3)
     def _():
-        first_blocks()
+        first_blocks(weight_whole)
+
+    @pl.when(z == 1)
+    def _():
+        weight_aside.wait_recv()
+        project_extra(0)
+        project_extra(1)
 
     arrived(2, 1 - y)
     project(2, 0)
@@ -655,35 +757,68 @@
 
     @pl.when(z == 3)
     def _():
-        first_blocks()
+        first_blocks(weight_less)
         finish(1, 1)
 
     project(2, 1)
+
+    @pl.when(z == 1)
+    def _():
+        project_extra(2)
+        finish_extra(0)
+        finish_extra(1)
+
     arrived(3, 1 - y)
     arrived(3, y)
     project(3, 0)
     finish(2, 1)
     project(3, 1)
+
+    @pl.when(z == 1)
+    def _():
+        project_extra(3)
+        finish_extra(2)
+
     finish(3, 0)
     finish(3, 1)
+
+    @pl.when(z == 1)
+    def _():
+        finish_extra(3)
+
 
     z_from = 2 * (h // 2) + z % 2
     for y_from in range(2):
         for h_from in range(4):
             rows = slice(h_from * 64, h_from * 64 + 64)
             spot = slice(y_from * 512, y_from * 512 + 512)
-            mine = (z_from == z) & (y_from == y) & (h_from == h)
-
-            @pl.when(jnp.logical_not(mine))
-            def _():
-                remote(
-                    final_out.at[0, 0],
-                    final_in.at[rows, spot],
+            here = (y_from == y) & (h_from == h)
+            remote_piece = jnp.logical_not((z_from == z) & here)
+            less = (z % 2 == 1) & (h == 2)
+
+            def piece(source, columns, sems):
+                return remote(
+                    source,
+                    final_in.at[rows, columns],
                     final_send.at[0, 0],
-                    final_recv.at[y_from * 4 + h_from],
+                    sems.at[y_from * 4 + h_from],
                     2 * z_from + y_from,
                     h_from,
-                ).wait_recv()
+                )
+
+            @pl.when(remote_piece & jnp.logical_not(less))
+            def _():
+                piece(final_out.at[0, 0], spot, final_recv).wait_recv()
+
+            @pl.when(remote_piece & less)
+            def _():
+                columns = slice(y_from * 512, y_from * 512 + 384)
+                piece(final_out.at[0, 0, :, pl.ds(0, 384)], columns, final_recv).wait_recv()
+
+            @pl.when(less & jnp.logical_not((z == 1) & here))
+            def _():
+                columns = slice(y_from * 512 + 384, y_from * 512 + 512)
+                piece(extra_out.at[0], columns, extra_final_recv).wait_recv()
 
     out_ref[...] = final_in[...]
 
@@ -694,8 +829,17 @@
 
     send_dep.wait_send()
     send_fade.wait_send()
-    for copy in weight_copies:
-        copy.wait_send()
+    @pl.when(z == 2)
+    def _():
+        for copy in weight_less:
+            copy.wait_send()
+        weight_aside.wait_send()
+
+    @pl.when(z != 2)
+    def _():
+        for copy in weight_whole:
+            copy.wait_send()
+
     for q in range(4):
         state_copies[q].wait_send()
 
@@ -711,14 +855,21 @@
         for side in range(2):
             for o in (1, 2, 3):
                 sum_copy(k, side, o).wait_send()
-            copy, stays = final_part(k, side)
-            if stays is None:
-                copy.wait_send()
-            else:
-
-                @pl.when(jnp.logical_not(stays))
+            for case, wide in final_cases(k, side):
+
+                @pl.when(case)
                 def _():
-                    copy.wait_send()
+                    final_part(k, side, wide).wait_send()
+
+    @pl.when(z == 1)
+    def _():
+        for k in range(4):
+            for o in (1, 2, 3):
+                extra_copy(k, o).wait_send()
+
+            @pl.when((h != 2) if k == 0 else (h >= 0))
+            def _():
+                extra_final(k).wait_send()
 
 
 def on_device_fast(
@@ -789,6 +940,16 @@
             dma((4, 2, 3)),
             dma((4, 2)),
             dma((8,)),
+            pltpu.VMEM((CHANNELS, 128), bf16),
+            pltpu.VMEM((4, SPAN, 128), bf16),
+            pltpu.VMEM((4, SPAN, 128), f32),
+            pltpu.VMEM((4, 3, 64, 128), bf16),
+            pltpu.VMEM((4, 64, 128), bf16),
+            dma((2,)),
+            dma((4, 3)),
+            dma((4, 3)),
+            dma((4,)),
+            dma((8,)),
         ],
         compiler_params=pltpu.CompilerParams(
             vmem_limit_bytes=56 * MIB, collective_id=0, has_side_effects=True

time: 127 us -> 127 us (level)
  no operation moved by 1% of the time
where the time goes in v6:
time: 127 us
  Pallas kernels  124 us (98%)
  local copies, waits for them, and re-layouts  3.55 us (3%)
    pallas_call x1, Pallas kernels, on_device_fast(): pl.pallas_call(fused_kernel, out_shape=jax.ShapeDtypeStruct((SPAN, 1024),...  124 us
    unnamed x2, local copies, waits for them, and re-layouts  3.55 us

profile of v6, /device:TPU:10, one launch (start us, length us, event | category | flops | bytes accessed | tf_op | source)
XLA Modules:
  0.0 127.1 jit_solution(1006201792282666589)
XLA Ops:
  0.0 1.7 %copy.12 = bf16[32,8,2,256]{3,1,2,0:T(8,128)(2,1)} copy(bf16[32,8,2,256]{3,2,1,0:T(2,128)(2,1)} %bitcast.6) | data formatting | bytes 524288
  1.7 123.6 %layer.1 = bf16[256,1024]{1,0:T(8,128)(2,1)} custom-call(bf16[256,2048]{1,0:T(8,128)(2,1)} %inner_ref.1, bf16[256,512]{1,0:T(8,128)(2,1)} %bitcast.5, f32[32,256]{1,0:T(8,128)} %step_ref.1, f32[1,32]{1,0:T(1,128)} %bitcast.9, s32[1,256]{1,0:T(1,128)} %bitcast.8, f32[4,2048]{1,0:T(4,128)} %filter_inner_ref.1, f32[4,2,256]{2,1,0:T(2,128)} %filter_state_ref.1, ...), custom_call_target="tpu_custom_call" | custom-call | tf_op jit(solution)/shard_map/layer/pallas_call | solution.py:893
  125.2 1.9 %copy.14 = bf16[256,1024]{1,0:T(8,128)(2,1)} copy(bf16[256,1024]{1,0:T(8,128)(2,1)} %layer.1) | data formatting | bytes 1048576
